TPU v7x, 32 devices: a whole 2x2x4 slice. The times are simulated.
32 devices in a mesh: groups: 2 (over x), tm: 16 (over z, y, core).
Axes of the slice: x: 2, y: 2, z: 4, core: 2. Of those that a mesh axis runs over, the one named last changes fastest.
Arguments:
- latent: bfloat16 [64, 8192], P('groups', 'tm'), parts along dimension 0, may hold values from -6 to 6
- w_in: bfloat16 [3, 3, 3, 16, 384], replicated, may hold values from -0.3125 to 0.3125
- b_in: float32 [384], replicated, may hold values from -3 to 3
- gain: float32 [384], replicated, may hold values from 0.1 to 1.9
- w_mid: bfloat16 [3, 3, 3, 384, 384], replicated, may hold values from -0.0625 to 0.0625
- b_mid: float32 [384], replicated, may hold values from -3 to 3
- w_time: bfloat16 [3, 384, 768], replicated, may hold values from -0.1875 to 0.1875
- b_time: float32 [768], replicated, may hold values from -3 to 3
Outputs:
- frames_up: bfloat16 [128, 16, 32, 384], P(('groups', 'tm')), parts along dimension 0
There are 2 independent parts, one for each index of `groups`. A program takes and returns all parts, laid end to end along the dimension named above; an argument that names none is the same for every part. Nothing has to cross between parts.
All inputs are finite; a program needn't handle non-finite values.
Results may differ from a plain program's by a relative error of at most 0.012.
Values may be sent and summed in bfloat16 or wider, within the bound.
No kernel may reach another device: no remote copies, remote signals or barrier semaphores. Data moves between devices by JAX's collectives and lax.ppermute only.
A program may use at most 128 MiB of HBM per device.

v0:
```python
import jax
import jax.numpy as jnp
from jax import lax
from jax.sharding import PartitionSpec as P

ZC = 16
C = 384
H = 16
W = 32


def passed_along(block, axis, distance):
    devices = range(lax.axis_size(axis))
    route = [(i - distance, i) for i in devices if i - distance in devices]
    return lax.ppermute(block, axis, route)


def conv_valid(padded, weight, bias, spatial):
    frames = padded.shape[0] - 2
    rows = padded.shape[1]
    inner = padded.shape[3]
    if spatial:
        margin = 1
        padded = jnp.pad(padded, ((0, 0), (1, 1), (margin, margin), (0, 0)))
        taps = 3
    else:
        taps = 1
    cols = padded.shape[2] - taps + 1
    total = jnp.zeros((frames * rows * cols, weight.shape[-1]), jnp.float32)
    for step_t in range(3):
        for step_h in range(taps):
            for step_w in range(taps):
                window = padded[
                    step_t : step_t + frames, step_h : step_h + rows, step_w : step_w + cols, :
                ]
                if spatial:
                    kernel = weight[step_t, step_h, step_w]
                else:
                    kernel = weight[step_t]
                total = total + jnp.dot(
                    window.reshape(-1, inner), kernel, preferred_element_type=jnp.float32
                )
    return (total + bias).reshape(frames, rows, cols, weight.shape[-1])


def conv_input(padded, weight, bias):
    frames = padded.shape[0] - 2
    rows = padded.shape[1]
    inner = padded.shape[3]
    margin = 1
    padded = jnp.pad(padded, ((0, 0), (1, 1), (margin, margin), (0, 0)))
    cols = padded.shape[2] - 2
    windows = []
    for step_t in range(3):
        for step_h in range(3):
            for step_w in range(3):
                windows.append(
                    padded[
                        step_t : step_t + frames, step_h : step_h + rows, step_w : step_w + cols, :
                    ]
                )
    stacked = jnp.concatenate(windows, axis=-1).reshape(frames * rows * cols, 27 * inner)
    total = jnp.dot(
        stacked, weight.reshape(27 * inner, weight.shape[-1]), preferred_element_type=jnp.float32
    )
    return (total + bias).reshape(frames, rows, cols, weight.shape[-1])


def activate(hidden, gain):
    values = hidden.astype(jnp.float32)
    scale = lax.rsqrt(jnp.mean(values * values, axis=-1, keepdims=True) + 1e-06)
    return jax.nn.silu(values * scale * gain).astype(jnp.bfloat16)


def per_device(latent, w_in, b_in, gain, w_mid, b_mid, w_time, b_time):
    owned = lax.all_to_all(latent, "tm", split_axis=0, concat_axis=1, tiled=True)
    frames = owned.shape[0]
    lat = owned.reshape(frames, H, W, ZC)
    earlier = passed_along(lat, "tm", 1)
    h0 = conv_input(jnp.concatenate([earlier, lat], axis=0), w_in, b_in).astype(jnp.bfloat16)
    act = activate(h0, gain)
    earlier_act = passed_along(act, "tm", 1)
    branch = conv_valid(jnp.concatenate([earlier_act, act], axis=0), w_mid, b_mid, True)
    h1 = (h0.astype(jnp.float32) + branch).astype(jnp.bfloat16)
    earlier_block = passed_along(h1, "tm", 1)
    up = conv_valid(jnp.concatenate([earlier_block, h1], axis=0), w_time, b_time, False)
    paired = up.reshape(frames, H, W, 2, C).transpose(0, 3, 1, 2, 4)
    return paired.reshape(2 * frames, H, W, C).astype(jnp.bfloat16)


def solution(mesh):
    return jax.shard_map(
        per_device,
        mesh=mesh,
        in_specs=(P("groups", "tm"), P(), P(), P(), P(), P(), P(), P()),
        out_specs=P(("groups", "tm"), None, None, None),
        check_vma=False,
    )
```

profile of v0, /device:TPU:10, one launch (start us, length us, event | category | flops | bytes accessed | tf_op | source)
XLA Modules:
  0.0 154.6 jit_solution(9824151615422119328)
XLA Ops:
  0.0 0.8 all_to_all.12
  0.8 11.1 %all_to_all.16 = bf16[16,2,512]{2,1,0:T(2,128)(2,1)S(1)} all-to-all(bf16[16,2,512]{2,1,0:T(2,128)(2,1)S(1)} %all_to_all.12), channel_id=1, replica_groups=mesh['groups'=2,'tm'=16] {'tm'}, dimensions={0} | all-to-all | bytes 65536 | tf_op jit(solution)/shard_map/all_to_all | solution.py:76
  12.2 2.0 %collective-permute-start = (bf16[2,16,32,16]{3,2,1,0:T(8,128)(2,1)S(1)}, bf16[2,16,32,16]{3,2,1,0:T(8,128)(2,1)S(1)}, u32[]{:S(2)}, u32[]{:S(2)}) collective-permute-start(bf16[2,16,32,16]{3,2,1,0:T(8,128)(2,1)S(1)} %reshape.157), channel_id=1, source_target_pairs={{0,1},{1,2},{2,3},{3,4},{4,5},{5,6},{6,7},{7,8},{8,9},{9,10},{10,1... | collective-permute-start | bytes 98312 | tf_op jit(solution)/shard_map/ppermute | solution.py:15
  14.6 6.2 %collective-permute-done = bf16[2,16,32,16]{3,2,1,0:T(8,128)(2,1)S(1)} collective-permute-done((bf16[2,16,32,16]{3,2,1,0:T(8,128)(2,1)S(1)}, bf16[2,16,32,16]{3,2,1,0:T(8,128)(2,1)S(1)}, u32[]{:S(2)}, u32[]{:S(2)}) %collective-permute-start) | collective-permute-done | bytes 32800 | tf_op jit(solution)/shard_map/ppermute | solution.py:15
  21.2 2.5 %pad_slice_fusion.26 = (bf16[2,16,32,16]{3,2,1,0:T(8,128)(2,1)}, bf16[2,16,32,16]{3,2,1,0:T(8,128)(2,1)}, bf16[2,16,32,16]{3,2,1,0:T(8,128)(2,1)}, bf16[2,16,32,...) fusion(bf16[4,16,32,16]{3,2,1,0:T(8,128)(2,1)S(1)} %constant_dy, ...), kind=kLoop, calls=%fused_computation.36 | loop fusion | bytes 688128 | tf_op jit(solution)/shard_map/slice | solution.py:58
  24.6 0.7 copy.90
  25.3 0.7 copy.91
  26.0 0.7 copy.92
  28.3 1.7 %copy.94 = bf16[1024,16]{0,1:T(8,128)(2,1)} copy(bf16[1024,16]{1,0:T(8,128)(2,1)} %bitcast.240) | data formatting | bytes 65536 | tf_op jit(solution)/shard_map/concatenate | solution.py:62
  30.0 1.7 %copy.70 = bf16[1024,16]{0,1:T(8,128)(2,1)} copy(bf16[1024,16]{1,0:T(8,128)(2,1)} %bitcast.239) | data formatting | bytes 65536 | tf_op jit(solution)/shard_map/concatenate | solution.py:62
  31.7 1.7 %copy.71 = bf16[1024,16]{0,1:T(8,128)(2,1)} copy(bf16[1024,16]{1,0:T(8,128)(2,1)} %bitcast.238) | data formatting | bytes 65536 | tf_op jit(solution)/shard_map/concatenate | solution.py:62
  33.4 1.7 %copy.72 = bf16[1024,16]{0,1:T(8,128)(2,1)} copy(bf16[1024,16]{1,0:T(8,128)(2,1)} %bitcast.237) | data formatting | bytes 65536 | tf_op jit(solution)/shard_map/concatenate | solution.py:62
  35.1 1.7 %copy.74 = bf16[1024,16]{0,1:T(8,128)(2,1)} copy(bf16[1024,16]{1,0:T(8,128)(2,1)} %bitcast.236) | data formatting | bytes 65536 | tf_op jit(solution)/shard_map/concatenate | solution.py:62
  36.7 1.7 %copy.75 = bf16[1024,16]{0,1:T(8,128)(2,1)} copy(bf16[1024,16]{1,0:T(8,128)(2,1)} %bitcast.235) | data formatting | bytes 65536 | tf_op jit(solution)/shard_map/concatenate | solution.py:62
  38.4 1.7 %copy.76 = bf16[1024,16]{0,1:T(8,128)(2,1)} copy(bf16[1024,16]{1,0:T(8,128)(2,1)} %bitcast.234) | data formatting | bytes 65536 | tf_op jit(solution)/shard_map/concatenate | solution.py:62
  40.1 0.7 copy.77
  58.4 2.0 %multiply_reduce_fusion = (f32[1024]{0:T(1024)S(1)}, f32[1024,384]{1,0:T(8,128)S(1)}) fusion(f32[384]{0:T(512)S(1)} %copy-done.44, bf16[1024,432]{0,1:T(8,128)(2,1)} %constant_dynamic-update-slice_fusion.2, bf16[432,384]{1,0:T(8,128)(2,1)S(1)} %bitcast.180), kind=kOutput, calls=%fused_computation.33 | convolution fusion | flops 341703680 | bytes 2795008 | tf_op jit(solution)/shard_map/dot_general | solution.py:63
  61.0 1.9 %collective-permute-start.1 = (bf16[2,16,32,384]{3,2,1,0:T(8,128)(2,1)S(1)}, bf16[2,16,32,384]{3,2,1,0:T(8,128)(2,1)S(1)}, u32[]{:S(2)}, u32[]{:S(2)}) collective-permute-start(bf16[2,16,32,384]{3,2,1,0:T(8,128)(2,1)S(1)} %multiply_convert_fusion.1), channel_id=1, source_target_pairs={{0,1},{1,2},{2,3},{3,4},{4,5},{5,6},{6,7},{7,8},{8,9},{9,10},{10,1... | collective-permute-start | bytes 2359304 | tf_op jit(solution)/shard_map/ppermute | solution.py:15
  62.9 3.0 %fusion.3 = f32[1024,384]{1,0:T(8,128)} fusion(f32[1024,384]{1,0:T(8,128)S(1)} %get-tuple-element.55, f32[384]{0:T(512)S(1)} %copy-done.43, f32[1024]{0:T(1024)S(1)} %add_rsqrt_fusion, bf16[3,3,3,384,384]{4,3,2,1,0:T(8,128)(2,1)} %param.12), kind=kOutput, calls=%fused_computation.63 | convolution fusion | flops 304742400 | bytes 3446272 | tf_op jit(solution)/shard_map/dot_general | solution.py:40
  65.9 9.3 %collective-permute-done.1 = bf16[2,16,32,384]{3,2,1,0:T(8,128)(2,1)S(1)} collective-permute-done((bf16[2,16,32,384]{3,2,1,0:T(8,128)(2,1)S(1)}, bf16[2,16,32,384]{3,2,1,0:T(8,128)(2,1)S(1)}, u32[]{:S(2)}, u32[]{:S(2)}) %collective-permute-start.1) | collective-permute-done | bytes 786464 | tf_op jit(solution)/shard_map/ppermute | solution.py:15
  75.4 2.1 %pad_slice_fusion.23 = (bf16[2,16,32,384]{3,2,1,0:T(8,128)(2,1)S(1)}, bf16[2,16,32,384]{3,2,1,0:T(8,128)(2,1)S(1)}, bf16[2,16,32,384]{3,2,1,0:T(8,128)(2,1)S(1)}...) fusion(bf16[4,16,32,384]{3,2,1,0:T(8,128)(2,1)S(1)} %pad_maximum_fusion), kind=kLoop, calls=%fused_computation.23 | loop fusion | bytes 5505024 | tf_op jit(solution)/shard_map/slice | solution.py:33
  77.6 6.2 %pad_slice_fusion = (bf16[2,16,32,384]{3,2,1,0:T(8,128)(2,1)}, bf16[2,16,32,384]{3,2,1,0:T(8,128)(2,1)}, bf16[2,16,32,384]{3,2,1,0:T(8,128)(2,1)}, bf16[2,16,32,...) fusion(bf16[4,16,32,384]{3,2,1,0:T(8,128)(2,1)S(1)} %pad_maximu, ...), kind=kLoop, calls=%fused_computation | loop fusion | bytes 16515072 | tf_op jit(solution)/shard_map/slice | solution.py:33
  88.3 1.8 %fusion.12 = f32[1024,384]{1,0:T(8,128)} fusion(bf16[1024,384]{1,0:T(8,128)(2,1)S(1)} %bitcast.210, bf16[3,3,3,384,384]{4,3,2,1,0:T(8,128)(2,1)S(1)} %bitcast.185), kind=kOutput, calls=%fused_computation.72 | convolution fusion | flops 301989888 | bytes 2654208 | tf_op jit(solution)/shard_map/dot_general | solution.py:40
  90.0 1.8 %fusion.59 = f32[1024,384]{1,0:T(8,128)} fusion(bf16[1024,384]{1,0:T(8,128)(2,1)S(1)} %bitcast.205, bf16[3,3,3,384,384]{4,3,2,1,0:T(8,128)(2,1)S(1)} %bitcast.185), kind=kOutput, calls=%fused_computation.119 | convolution fusion | flops 301989888 | bytes 2654208 | tf_op jit(solution)/shard_map/dot_general | solution.py:40
  91.8 1.8 %fusion.57 = f32[1024,384]{1,0:T(8,128)} fusion(bf16[1024,384]{1,0:T(8,128)(2,1)S(1)} %bitcast.204, bf16[3,3,3,384,384]{4,3,2,1,0:T(8,128)(2,1)S(1)} %bitcast.185), kind=kOutput, calls=%fused_computation.117 | convolution fusion | flops 301989888 | bytes 2654208 | tf_op jit(solution)/shard_map/dot_general | solution.py:40
  93.6 1.8 %fusion.55 = f32[1024,384]{1,0:T(8,128)} fusion(bf16[1024,384]{1,0:T(8,128)(2,1)S(1)} %bitcast.203, bf16[3,3,3,384,384]{4,3,2,1,0:T(8,128)(2,1)S(1)} %bitcast.185), kind=kOutput, calls=%fused_computation.115 | convolution fusion | flops 301989888 | bytes 2654208 | tf_op jit(solution)/shard_map/dot_general | solution.py:40
  95.4 1.8 %fusion.51 = f32[1024,384]{1,0:T(8,128)} fusion(bf16[1024,384]{1,0:T(8,128)(2,1)S(1)} %bitcast.202, bf16[3,3,3,384,384]{4,3,2,1,0:T(8,128)(2,1)S(1)} %bitcast.185), kind=kOutput, calls=%fused_computation.111 | convolution fusion | flops 301989888 | bytes 2654208 | tf_op jit(solution)/shard_map/dot_general | solution.py:40
  97.2 1.8 %fusion.49 = f32[1024,384]{1,0:T(8,128)} fusion(bf16[1024,384]{1,0:T(8,128)(2,1)S(1)} %bitcast.201, bf16[3,3,3,384,384]{4,3,2,1,0:T(8,128)(2,1)S(1)} %bitcast.185), kind=kOutput, calls=%fused_computation.109 | convolution fusion | flops 301989888 | bytes 2654208 | tf_op jit(solution)/shard_map/dot_general | solution.py:40
  99.1 1.8 %fusion.47 = f32[1024,384]{1,0:T(8,128)} fusion(bf16[1024,384]{1,0:T(8,128)(2,1)S(1)} %bitcast.200, bf16[3,3,3,384,384]{4,3,2,1,0:T(8,128)(2,1)S(1)} %bitcast.185), kind=kOutput, calls=%fused_computation.107 | convolution fusion | flops 301989888 | bytes 2654208 | tf_op jit(solution)/shard_map/dot_general | solution.py:40
  100.9 1.9 %fusion.45 = f32[1024,384]{1,0:T(8,128)} fusion(bf16[1024,384]{1,0:T(8,128)(2,1)S(1)} %bitcast.199, bf16[3,3,3,384,384]{4,3,2,1,0:T(8,128)(2,1)S(1)} %bitcast.185), kind=kOutput, calls=%fused_computation.105 | convolution fusion | flops 301989888 | bytes 2654208 | tf_op jit(solution)/shard_map/dot_general | solution.py:40
  102.7 1.8 %fusion.43 = f32[1024,384]{1,0:T(8,128)} fusion(bf16[1024,384]{1,0:T(8,128)(2,1)S(1)} %bitcast.198, bf16[3,3,3,384,384]{4,3,2,1,0:T(8,128)(2,1)S(1)} %bitcast.185), kind=kOutput, calls=%fused_computation.103 | convolution fusion | flops 301989888 | bytes 2654208 | tf_op jit(solution)/shard_map/dot_general | solution.py:40
  104.5 1.8 %fusion.41 = f32[1024,384]{1,0:T(8,128)} fusion(bf16[1024,384]{1,0:T(8,128)(2,1)S(1)} %bitcast.197, bf16[3,3,3,384,384]{4,3,2,1,0:T(8,128)(2,1)S(1)} %bitcast.185), kind=kOutput, calls=%fused_computation.101 | convolution fusion | flops 301989888 | bytes 2654208 | tf_op jit(solution)/shard_map/dot_general | solution.py:40
  106.3 1.8 %fusion.39 = f32[1024,384]{1,0:T(8,128)} fusion(bf16[1024,384]{1,0:T(8,128)(2,1)S(1)} %bitcast.196, bf16[3,3,3,384,384]{4,3,2,1,0:T(8,128)(2,1)S(1)} %bitcast.185), kind=kOutput, calls=%fused_computation.99 | convolution fusion | flops 301989888 | bytes 2654208 | tf_op jit(solution)/shard_map/dot_general | solution.py:40
  108.1 1.8 %fusion.37 = f32[1024,384]{1,0:T(8,128)} fusion(bf16[1024,384]{1,0:T(8,128)(2,1)S(1)} %bitcast.195, bf16[3,3,3,384,384]{4,3,2,1,0:T(8,128)(2,1)S(1)} %bitcast.185), kind=kOutput, calls=%fused_computation.97 | convolution fusion | flops 301989888 | bytes 2654208 | tf_op jit(solution)/shard_map/dot_general | solution.py:40
  109.9 1.8 %fusion.33 = f32[1024,384]{1,0:T(8,128)} fusion(bf16[1024,384]{1,0:T(8,128)(2,1)S(1)} %bitcast.194, bf16[3,3,3,384,384]{4,3,2,1,0:T(8,128)(2,1)S(1)} %bitcast.185), kind=kOutput, calls=%fused_computation.93 | convolution fusion | flops 301989888 | bytes 2654208 | tf_op jit(solution)/shard_map/dot_general | solution.py:40
  111.7 1.8 %fusion.31 = f32[1024,384]{1,0:T(8,128)} fusion(bf16[1024,384]{1,0:T(8,128)(2,1)S(1)} %bitcast.193, bf16[3,3,3,384,384]{4,3,2,1,0:T(8,128)(2,1)S(1)} %bitcast.185), kind=kOutput, calls=%fused_computation.91 | convolution fusion | flops 301989888 | bytes 2654208 | tf_op jit(solution)/shard_map/dot_general | solution.py:40
  113.5 2.1 %fusion.29 = f32[1024,384]{1,0:T(8,128)} fusion(bf16[1024,384]{1,0:T(8,128)(2,1)S(1)} %bitcast.192, bf16[3,3,3,384,384]{4,3,2,1,0:T(8,128)(2,1)S(1)} %bitcast.185), kind=kOutput, calls=%fused_computation.89 | convolution fusion | flops 301989888 | bytes 2654208 | tf_op jit(solution)/shard_map/dot_general | solution.py:40
  115.5 1.9 %fusion.27 = f32[1024,384]{1,0:T(8,128)} fusion(bf16[1024,384]{1,0:T(8,128)(2,1)S(1)} %bitcast.191, bf16[3,3,3,384,384]{4,3,2,1,0:T(8,128)(2,1)S(1)} %bitcast.185), kind=kOutput, calls=%fused_computation.87 | convolution fusion | flops 301989888 | bytes 2654208 | tf_op jit(solution)/shard_map/dot_general | solution.py:40
  117.4 1.9 %fusion.25 = f32[1024,384]{1,0:T(8,128)} fusion(bf16[1024,384]{1,0:T(8,128)(2,1)S(1)} %bitcast.190, bf16[3,3,3,384,384]{4,3,2,1,0:T(8,128)(2,1)S(1)} %bitcast.185), kind=kOutput, calls=%fused_computation.85 | convolution fusion | flops 301989888 | bytes 2654208 | tf_op jit(solution)/shard_map/dot_general | solution.py:40
  119.3 1.8 %fusion.23 = f32[1024,384]{1,0:T(8,128)} fusion(bf16[1024,384]{1,0:T(8,128)(2,1)S(1)} %bitcast.189, bf16[3,3,3,384,384]{4,3,2,1,0:T(8,128)(2,1)S(1)} %bitcast.185), kind=kOutput, calls=%fused_computation.83 | convolution fusion | flops 301989888 | bytes 2654208 | tf_op jit(solution)/shard_map/dot_general | solution.py:40
  121.0 1.8 %fusion.21 = f32[1024,384]{1,0:T(8,128)} fusion(bf16[1024,384]{1,0:T(8,128)(2,1)S(1)} %bitcast.188, bf16[3,3,3,384,384]{4,3,2,1,0:T(8,128)(2,1)S(1)} %bitcast.185), kind=kOutput, calls=%fused_computation.81 | convolution fusion | flops 301989888 | bytes 2654208 | tf_op jit(solution)/shard_map/dot_general | solution.py:40
  122.8 13.2 %add_add_fusion = f32[1024,384]{1,0:T(8,128)S(1)} fusion(f32[1024,384]{1,0:T(8,128)} %fusion.12, f32[1024,384]{1,0:T(8,128)S(1)} %fusion.14, f32[1024,384]{1,0:T(8,128)S(1)} %fusion.16, f32[1024,384]{1,0:T(8,128)} %fusion.3, f32[1024,384]{1,0:T(8,128)S(1)} %fusion.19, f32[1024,384]{1,0:T(8,128)} %fusion.21, f32[1024,384]{1,0:T(8,128)} %fusion.23, ...), kind=kOutput, calls=%fused_computation.30 | convolution fusion | flops 312606720 | bytes 43550208 | tf_op jit(solution)/shard_map/dot_general | solution.py:40
  136.3 2.1 %collective-permute-start.2 = (bf16[2,16,32,384]{3,2,1,0:T(8,128)(2,1)S(1)}, bf16[2,16,32,384]{3,2,1,0:T(8,128)(2,1)S(1)}, u32[]{:S(2)}, u32[]{:S(2)}) collective-permute-start(bf16[2,16,32,384]{3,2,1,0:T(8,128)(2,1)S(1)} %add_convert_fusion.2), channel_id=1, source_target_pairs={{0,1},{1,2},{2,3},{3,4},{4,5},{5,6},{6,7},{7,8},{8,9},{9,10},{10,1... | collective-permute-start | bytes 2359304 | tf_op jit(solution)/shard_map/ppermute | solution.py:15
  138.4 1.0 fusion.1
  139.4 11.3 %collective-permute-done.2 = bf16[2,16,32,384]{3,2,1,0:T(8,128)(2,1)S(1)} collective-permute-done((bf16[2,16,32,384]{3,2,1,0:T(8,128)(2,1)S(1)}, bf16[2,16,32,384]{3,2,1,0:T(8,128)(2,1)S(1)}, u32[]{:S(2)}, u32[]{:S(2)}) %collective-permute-start.2) | collective-permute-done | bytes 786464 | tf_op jit(solution)/shard_map/ppermute | solution.py:15
  150.8 1.0 fusion.5
  151.8 1.0 add_convert_fusion
  153.2 1.4 copy.68
  (158 shorter events, 26.8 us)
Async XLA Ops:
  0.0 58.4 %copy-start = (bf16[3,3,3,16,384]{4,3,2,1,0:T(8,128)(2,1)S(1)}, bf16[3,3,3,16,384]{4,3,2,1,0:T(8,128)(2,1)}, u32[]{:S(2)}) copy-start(bf16[3,3,3,16,384]{4,3,2,1,0:T(8,128)(2,1)} %param.9) | copy-start | bytes 995332
  12.2 8.6 %collective-permute-start = (bf16[2,16,32,16]{3,2,1,0:T(8,128)(2,1)S(1)}, bf16[2,16,32,16]{3,2,1,0:T(8,128)(2,1)S(1)}, u32[]{:S(2)}, u32[]{:S(2)}) collective-permute-start(bf16[2,16,32,16]{3,2,1,0:T(8,128)(2,1)S(1)} %reshape.157), channel_id=1, source_target_pairs={{0,1},{1,2},{2,3},{3,4},{4,5},{5,6},{6,7},{7,8},{8,9},{9,10},{10,1... | collective-permute-start | bytes 98312 | tf_op jit(solution)/shard_map/ppermute | solution.py:15
  26.0 14.0 %copy-start.27 = (bf16[2,16,32,16]{3,2,1,0:T(8,128)(2,1)S(1)}, bf16[2,16,32,16]{3,2,1,0:T(8,128)(2,1)}, u32[]{:S(2)}) copy-start(bf16[2,16,32,16]{3,2,1,0:T(8,128)(2,1)} %get-tuple-element.36) | copy-start | bytes 98308
  26.8 14.0 %copy-start.26 = (bf16[2,16,32,16]{3,2,1,0:T(8,128)(2,1)S(1)}, bf16[2,16,32,16]{3,2,1,0:T(8,128)(2,1)}, u32[]{:S(2)}) copy-start(bf16[2,16,32,16]{3,2,1,0:T(8,128)(2,1)} %get-tuple-element.37) | copy-start | bytes 98308
  27.5 13.4 %copy-start.25 = (bf16[2,16,32,16]{3,2,1,0:T(8,128)(2,1)S(1)}, bf16[2,16,32,16]{3,2,1,0:T(8,128)(2,1)}, u32[]{:S(2)}) copy-start(bf16[2,16,32,16]{3,2,1,0:T(8,128)(2,1)} %get-tuple-element.38) | copy-start | bytes 98308
  27.6 13.5 %copy-start.24 = (bf16[2,16,32,16]{3,2,1,0:T(8,128)(2,1)S(1)}, bf16[2,16,32,16]{3,2,1,0:T(8,128)(2,1)}, u32[]{:S(2)}) copy-start(bf16[2,16,32,16]{3,2,1,0:T(8,128)(2,1)} %get-tuple-element.39) | copy-start | bytes 98308
  28.3 13.0 %copy-start.23 = (bf16[2,16,32,16]{3,2,1,0:T(8,128)(2,1)S(1)}, bf16[2,16,32,16]{3,2,1,0:T(8,128)(2,1)}, u32[]{:S(2)}) copy-start(bf16[2,16,32,16]{3,2,1,0:T(8,128)(2,1)} %get-tuple-element.40) | copy-start | bytes 98308
  30.0 11.4 %copy-start.22 = (bf16[2,16,32,16]{3,2,1,0:T(8,128)(2,1)S(1)}, bf16[2,16,32,16]{3,2,1,0:T(8,128)(2,1)}, u32[]{:S(2)}) copy-start(bf16[2,16,32,16]{3,2,1,0:T(8,128)(2,1)} %get-tuple-element.41) | copy-start | bytes 98308
  31.7 9.8 %copy-start.21 = (bf16[2,16,32,16]{3,2,1,0:T(8,128)(2,1)S(1)}, bf16[2,16,32,16]{3,2,1,0:T(8,128)(2,1)}, u32[]{:S(2)}) copy-start(bf16[2,16,32,16]{3,2,1,0:T(8,128)(2,1)} %get-tuple-element.42) | copy-start | bytes 98308
  40.8 1.4 copy-start.39
  40.9 2.0 %copy-start.40 = (bf16[1024,16]{0,1:T(8,128)(2,1)S(1)}, bf16[1024,16]{0,1:T(8,128)(2,1)}, u32[]{:S(2)}) copy-start(bf16[1024,16]{0,1:T(8,128)(2,1)} %copy.71) | copy-start | bytes 98308
  40.9 2.6 %copy-start.38 = (bf16[1024,16]{0,1:T(8,128)(2,1)S(1)}, bf16[1024,16]{0,1:T(8,128)(2,1)}, u32[]{:S(2)}) copy-start(bf16[1024,16]{0,1:T(8,128)(2,1)} %copy.72) | copy-start | bytes 98308
  41.0 3.2 %copy-start.33 = (bf16[1024,16]{0,1:T(8,128)(2,1)S(1)}, bf16[1024,16]{0,1:T(8,128)(2,1)}, u32[]{:S(2)}) copy-start(bf16[1024,16]{0,1:T(8,128)(2,1)} %copy.73) | copy-start | bytes 98308
  41.0 3.8 %copy-start.37 = (bf16[1024,16]{0,1:T(8,128)(2,1)S(1)}, bf16[1024,16]{0,1:T(8,128)(2,1)}, u32[]{:S(2)}) copy-start(bf16[1024,16]{0,1:T(8,128)(2,1)} %copy.74) | copy-start | bytes 98308
  41.1 4.3 %copy-start.36 = (bf16[1024,16]{0,1:T(8,128)(2,1)S(1)}, bf16[1024,16]{0,1:T(8,128)(2,1)}, u32[]{:S(2)}) copy-start(bf16[1024,16]{0,1:T(8,128)(2,1)} %copy.75) | copy-start | bytes 98308
  41.1 4.9 %copy-start.35 = (bf16[1024,16]{0,1:T(8,128)(2,1)S(1)}, bf16[1024,16]{0,1:T(8,128)(2,1)}, u32[]{:S(2)}) copy-start(bf16[1024,16]{0,1:T(8,128)(2,1)} %copy.76) | copy-start | bytes 98308
  41.1 5.5 %copy-start.34 = (bf16[1024,16]{0,1:T(8,128)(2,1)S(1)}, bf16[1024,16]{0,1:T(8,128)(2,1)}, u32[]{:S(2)}) copy-start(bf16[1024,16]{0,1:T(8,128)(2,1)} %copy.77) | copy-start | bytes 98308
  41.2 8.5 %copy-start.32 = (bf16[1024,16]{0,1:T(8,128)(2,1)S(1)}, bf16[1024,16]{0,1:T(8,128)(2,1)}, u32[]{:S(2)}) copy-start(bf16[1024,16]{0,1:T(8,128)(2,1)} %copy.82) | copy-start | bytes 98308
  41.5 13.2 %copy-start.31 = (bf16[1024,16]{0,1:T(8,128)(2,1)S(1)}, bf16[1024,16]{0,1:T(8,128)(2,1)}, u32[]{:S(2)}) copy-start(bf16[1024,16]{0,1:T(8,128)(2,1)} %copy.90) | copy-start | bytes 98308
  41.5 14.4 %copy-start.29 = (bf16[1024,16]{0,1:T(8,128)(2,1)S(1)}, bf16[1024,16]{0,1:T(8,128)(2,1)}, u32[]{:S(2)}) copy-start(bf16[1024,16]{0,1:T(8,128)(2,1)} %copy.91) | copy-start | bytes 98308
  41.6 14.9 %copy-start.28 = (bf16[1024,16]{0,1:T(8,128)(2,1)S(1)}, bf16[1024,16]{0,1:T(8,128)(2,1)}, u32[]{:S(2)}) copy-start(bf16[1024,16]{0,1:T(8,128)(2,1)} %copy.92) | copy-start | bytes 98308
  41.6 16.1 %copy-start.30 = (bf16[1024,16]{0,1:T(8,128)(2,1)S(1)}, bf16[1024,16]{0,1:T(8,128)(2,1)}, u32[]{:S(2)}) copy-start(bf16[1024,16]{0,1:T(8,128)(2,1)} %copy.94) | copy-start | bytes 98308
  41.6 16.7 %copy-start.44 = (f32[384]{0:T(512)S(1)}, f32[384]{0:T(512)}, u32[]{:S(2)}) copy-start(f32[384]{0:T(512)} %param.10) | copy-start | bytes 4612
  58.4 2.1 %copy-start.43 = (f32[384]{0:T(512)S(1)}, f32[384]{0:T(512)}, u32[]{:S(2)}) copy-start(f32[384]{0:T(512)} %param.11) | copy-start | bytes 4612
  61.0 14.2 %collective-permute-start.1 = (bf16[2,16,32,384]{3,2,1,0:T(8,128)(2,1)S(1)}, bf16[2,16,32,384]{3,2,1,0:T(8,128)(2,1)S(1)}, u32[]{:S(2)}, u32[]{:S(2)}) collective-permute-start(bf16[2,16,32,384]{3,2,1,0:T(8,128)(2,1)S(1)} %multiply_convert_fusion.1), channel_id=1, source_target_pairs={{0,1},{1,2},{2,3},{3,4},{4,5},{5,6},{6,7},{7,8},{8,9},{9,10},{10,1... | collective-permute-start | bytes 2359304 | tf_op jit(solution)/shard_map/ppermute | solution.py:15
  75.4 8.5 %slice-start = ((s8[7962624]{0:T(1024)(128)(4,1)}), s8[4194304]{0:T(1024)(128)(4,1)S(1)}, s32[]{:S(2)}) async-start(s8[7962624]{0:T(1024)(128)(4,1)} %bitcast.184), calls=%async_computation.1 | async-start | bytes 8388608
  77.5 6.3 %slice-start.1 = ((s8[7962624]{0:T(1024)(128)(4,1)}), s8[3768320]{0:T(1024)(128)(4,1)S(1)}, s32[]{:S(2)}) async-start(s8[7962624]{0:T(1024)(128)(4,1)} %bitcast.184), calls=%async_computation.2 | async-start | bytes 7536640
  87.1 1.2 copy-start.18
  88.2 1.8 %copy-start.17 = (bf16[2,16,32,384]{3,2,1,0:T(8,128)(2,1)S(1)}, bf16[2,16,32,384]{3,2,1,0:T(8,128)(2,1)}, u32[]{:S(2)}) copy-start(bf16[2,16,32,384]{3,2,1,0:T(8,128)(2,1)} %get-tuple-element.6) | copy-start | bytes 2359300
  90.0 1.8 %copy-start.16 = (bf16[2,16,32,384]{3,2,1,0:T(8,128)(2,1)S(1)}, bf16[2,16,32,384]{3,2,1,0:T(8,128)(2,1)}, u32[]{:S(2)}) copy-start(bf16[2,16,32,384]{3,2,1,0:T(8,128)(2,1)} %get-tuple-element.7) | copy-start | bytes 2359300
  91.8 1.8 %copy-start.15 = (bf16[2,16,32,384]{3,2,1,0:T(8,128)(2,1)S(1)}, bf16[2,16,32,384]{3,2,1,0:T(8,128)(2,1)}, u32[]{:S(2)}) copy-start(bf16[2,16,32,384]{3,2,1,0:T(8,128)(2,1)} %get-tuple-element.8) | copy-start | bytes 2359300
  93.6 1.8 %copy-start.14 = (bf16[2,16,32,384]{3,2,1,0:T(8,128)(2,1)S(1)}, bf16[2,16,32,384]{3,2,1,0:T(8,128)(2,1)}, u32[]{:S(2)}) copy-start(bf16[2,16,32,384]{3,2,1,0:T(8,128)(2,1)} %get-tuple-element.9) | copy-start | bytes 2359300
  95.4 1.8 %copy-start.13 = (bf16[2,16,32,384]{3,2,1,0:T(8,128)(2,1)S(1)}, bf16[2,16,32,384]{3,2,1,0:T(8,128)(2,1)}, u32[]{:S(2)}) copy-start(bf16[2,16,32,384]{3,2,1,0:T(8,128)(2,1)} %get-tuple-element.10) | copy-start | bytes 2359300
  97.2 1.8 %copy-start.12 = (bf16[2,16,32,384]{3,2,1,0:T(8,128)(2,1)S(1)}, bf16[2,16,32,384]{3,2,1,0:T(8,128)(2,1)}, u32[]{:S(2)}) copy-start(bf16[2,16,32,384]{3,2,1,0:T(8,128)(2,1)} %get-tuple-element.11) | copy-start | bytes 2359300
  99.1 1.8 %copy-start.11 = (bf16[2,16,32,384]{3,2,1,0:T(8,128)(2,1)S(1)}, bf16[2,16,32,384]{3,2,1,0:T(8,128)(2,1)}, u32[]{:S(2)}) copy-start(bf16[2,16,32,384]{3,2,1,0:T(8,128)(2,1)} %get-tuple-element.12) | copy-start | bytes 2359300
  100.9 1.9 %copy-start.10 = (bf16[2,16,32,384]{3,2,1,0:T(8,128)(2,1)S(1)}, bf16[2,16,32,384]{3,2,1,0:T(8,128)(2,1)}, u32[]{:S(2)}) copy-start(bf16[2,16,32,384]{3,2,1,0:T(8,128)(2,1)} %get-tuple-element.13) | copy-start | bytes 2359300
  102.7 1.8 %copy-start.9 = (bf16[2,16,32,384]{3,2,1,0:T(8,128)(2,1)S(1)}, bf16[2,16,32,384]{3,2,1,0:T(8,128)(2,1)}, u32[]{:S(2)}) copy-start(bf16[2,16,32,384]{3,2,1,0:T(8,128)(2,1)} %get-tuple-element.14) | copy-start | bytes 2359300
  104.5 1.8 %copy-start.8 = (bf16[2,16,32,384]{3,2,1,0:T(8,128)(2,1)S(1)}, bf16[2,16,32,384]{3,2,1,0:T(8,128)(2,1)}, u32[]{:S(2)}) copy-start(bf16[2,16,32,384]{3,2,1,0:T(8,128)(2,1)} %get-tuple-element.15) | copy-start | bytes 2359300
  106.3 1.8 %copy-start.7 = (bf16[2,16,32,384]{3,2,1,0:T(8,128)(2,1)S(1)}, bf16[2,16,32,384]{3,2,1,0:T(8,128)(2,1)}, u32[]{:S(2)}) copy-start(bf16[2,16,32,384]{3,2,1,0:T(8,128)(2,1)} %get-tuple-element.16) | copy-start | bytes 2359300
  108.1 1.8 %copy-start.6 = (bf16[2,16,32,384]{3,2,1,0:T(8,128)(2,1)S(1)}, bf16[2,16,32,384]{3,2,1,0:T(8,128)(2,1)}, u32[]{:S(2)}) copy-start(bf16[2,16,32,384]{3,2,1,0:T(8,128)(2,1)} %get-tuple-element.17) | copy-start | bytes 2359300
  109.9 1.8 %copy-start.5 = (bf16[2,16,32,384]{3,2,1,0:T(8,128)(2,1)S(1)}, bf16[2,16,32,384]{3,2,1,0:T(8,128)(2,1)}, u32[]{:S(2)}) copy-start(bf16[2,16,32,384]{3,2,1,0:T(8,128)(2,1)} %get-tuple-element.18) | copy-start | bytes 2359300
  111.6 1.8 %copy-start.4 = (bf16[2,16,32,384]{3,2,1,0:T(8,128)(2,1)S(1)}, bf16[2,16,32,384]{3,2,1,0:T(8,128)(2,1)}, u32[]{:S(2)}) copy-start(bf16[2,16,32,384]{3,2,1,0:T(8,128)(2,1)} %get-tuple-element.19) | copy-start | bytes 2359300
  113.5 2.1 %copy-start.3 = (bf16[2,16,32,384]{3,2,1,0:T(8,128)(2,1)S(1)}, bf16[2,16,32,384]{3,2,1,0:T(8,128)(2,1)}, u32[]{:S(2)}) copy-start(bf16[2,16,32,384]{3,2,1,0:T(8,128)(2,1)} %get-tuple-element.20) | copy-start | bytes 2359300
  115.5 1.9 %copy-start.2 = (bf16[2,16,32,384]{3,2,1,0:T(8,128)(2,1)S(1)}, bf16[2,16,32,384]{3,2,1,0:T(8,128)(2,1)}, u32[]{:S(2)}) copy-start(bf16[2,16,32,384]{3,2,1,0:T(8,128)(2,1)} %get-tuple-element.21) | copy-start | bytes 2359300
  121.0 1.8 %copy-start.42 = (f32[384]{0:T(512)S(1)}, f32[384]{0:T(512)}, u32[]{:S(2)}) copy-start(f32[384]{0:T(512)} %param.13) | copy-start | bytes 4612
  136.0 2.4 %copy-start.20 = (bf16[3,384,768]{2,1,0:T(8,128)(2,1)S(1)}, bf16[3,384,768]{2,1,0:T(8,128)(2,1)}, u32[]{:S(2)}) copy-start(bf16[3,384,768]{2,1,0:T(8,128)(2,1)} %param.14) | copy-start | bytes 5308420
  136.3 14.3 %collective-permute-start.2 = (bf16[2,16,32,384]{3,2,1,0:T(8,128)(2,1)S(1)}, bf16[2,16,32,384]{3,2,1,0:T(8,128)(2,1)S(1)}, u32[]{:S(2)}, u32[]{:S(2)}) collective-permute-start(bf16[2,16,32,384]{3,2,1,0:T(8,128)(2,1)S(1)} %add_convert_fusion.2), channel_id=1, source_target_pairs={{0,1},{1,2},{2,3},{3,4},{4,5},{5,6},{6,7},{7,8},{8,9},{9,10},{10,1... | collective-permute-start | bytes 2359304 | tf_op jit(solution)/shard_map/ppermute | solution.py:15
  153.2 1.4 copy-start.1
  (2 other events, 2.1 us)
where the time goes:
time: 155 us
  matrix products  59.3 us (38%)
  local copies, waits for them, and re-layouts  49.7 us (32%)
  waiting for transfers between devices  26.8 us (17%)
  blocking collectives  11.1 us (7%)
  starting transfers between devices  6 us (4%)
    dot_general x30, matrix products, conv_valid(): jnp.dot(window.reshape(-1, inner), kernel, preferred_element_type=jnp.flo...  57.3 us
    ppermute x3, waiting for transfers between devices, passed_along(): return lax.ppermute(block, axis, route)  26.8 us
    concatenate x29, local copies, waits for them, and re-layouts, conv_input(): jnp.concatenate(windows, axis=-1).reshape(frames * rows * cols, 27 * inner)  18.7 us
    unnamed x121, local copies, waits for them, and re-layouts  16.8 us
    all_to_all x1, blocking collectives, per_device(): lax.all_to_all(latent, 'tm', split_axis=0, concat_axis=1, tiled=True)  11.1 us
    slice x2, local copies, waits for them, and re-layouts, conv_valid(): padded[step_t:step_t + frames, step_h:step_h + rows, step_w:step_w + cols...  8.35 us
    ppermute x3, starting transfers between devices, passed_along(): return lax.ppermute(block, axis, route)  6 us
  transfers between devices with their start and end apart: 3, of which 3 were waited for; matrix products, arithmetic and copies ran while one was open for 3% of the time, Pallas kernels for 0%

commit v1 on v0

v1 whole, which is shorter than its diff:
```python
import jax
import jax.numpy as jnp
from jax import lax
from jax.experimental import pallas as pl
from jax.experimental.pallas import tpu as pltpu
from jax.sharding import PartitionSpec as P

ZC = 16
C = 384
H = 16
W = 32
NT = 2
LATF = NT + 6
ACTF = NT + 4
MIDF = NT + 2
PAIRS = W // 2
LANES = 640
K3 = 3 * C
F32 = jnp.float32
BF16 = jnp.bfloat16


def kernel(
    x_ref, win_ref, bin_ref, gain_ref, wm_hbm, bmid_ref, wt_hbm, btime_ref, out_ref,
    wm, wt, toep, lhs, h0_s, vt, v_s, u_s, m_s, y_s, tr, hcat, sem_m, sem_t,
):
    copy_m = pltpu.make_async_copy(wm_hbm, wm, sem_m)
    copy_t = pltpu.make_async_copy(wt_hbm, wt, sem_t)
    copy_m.start()
    copy_t.start()
    first = lax.axis_index("tm") * NT

    toep[...] = jnp.zeros_like(toep)
    for dt in range(3):
        for dh in range(3):
            base = dt * 128 + dh * 64 if dh < 2 else 384 + dt * 128
            for j in range(4):
                for o in range(2):
                    dw = j - o
                    if 0 <= dw <= 2:
                        tap = ((dt * 3 + dh) * 3 + dw) * ZC
                        toep[base + 16 * j : base + 16 * j + 16, o * C : (o + 1) * C] = win_ref[
                            tap : tap + ZC, :
                        ]

    x = x_ref[...].astype(F32)
    row = lax.broadcasted_iota(jnp.int32, x.shape, 0) % H
    lane = lax.broadcasted_iota(jnp.int32, x.shape, 1) % 128
    above = jnp.where(row == 0, 0.0, pltpu.roll(x, 1, 0))
    below = jnp.where(row == H - 1, 0.0, pltpu.roll(x, x.shape[0] - 1, 0))
    for q in range(4):
        left = (LANES - 32 * q) % LANES
        mid = (LANES + 64 - 32 * q) % LANES
        a0 = pltpu.roll(above, left, 1) if left else above
        a1 = pltpu.roll(x, mid, 1) if mid else x
        a2 = pltpu.roll(below, left, 1) if left else below
        pair = jnp.where(lane < 64, a0, a1).astype(BF16)
        last = a2.astype(BF16)
        for g in range(4):
            for dt in range(3):
                rows = slice(g * ACTF * H, (g + 1) * ACTF * H)
                src = slice(dt * H, dt * H + ACTF * H)
                lhs[q, rows, dt * 128 : dt * 128 + 128] = pair[src, g * 128 : (g + 1) * 128]
                lhs[q, rows, 384 + dt * 128 : 512 + dt * 128] = last[src, g * 128 : (g + 1) * 128]

    for kt in range(4):
        for t in range(2):
            vt[kt, 0, t, 0] = jnp.zeros((H, K3), BF16)
            vt[kt, 1, t, PAIRS] = jnp.zeros((H, K3), BF16)
    b_in = bin_ref[...].reshape(1, C)
    gain = gain_ref[...].reshape(1, C)
    sub = lax.broadcasted_iota(jnp.int32, (8, C), 0)
    keep = [jnp.where(first - 4 + f >= 0, 1.0, 0.0).astype(F32) for f in range(ACTF)]

    @pl.loop(0, 4)
    def _(q):
        y = jnp.dot(lhs[q], toep[...], preferred_element_type=F32)
        for o in range(2):
            for g in range(4):
                part = y[g * ACTF * H : (g + 1) * ACTF * H, o * C : (o + 1) * C] + b_in
                hb = part.astype(BF16)
                for f in range(2, ACTF):
                    h0_s[f - 2, o, 4 * g + q] = hb[f * H : (f + 1) * H]
                h = hb.astype(F32)
                scale = lax.rsqrt(jnp.mean(h * h, axis=-1, keepdims=True) + 1e-06)
                v = h * scale * gain
                a = 0.5 * v * (1.0 + jnp.tanh(0.5 * v))
                d = [a[f * H : (f + 1) * H] * keep[f] for f in range(ACTF)]
                for t in range(2):
                    d0, d1, d2, d3 = d[2 * t : 2 * t + 4]
                    for kt, r in enumerate((d0 - d2, 0.5 * (d1 + d2), 0.5 * (d2 - d1), d1 - d3)):
                        lo, hi = r[:8], r[8:]
                        lo1, hi1 = pltpu.roll(lo, 1, 0), pltpu.roll(hi, 1, 0)
                        lo7, hi7 = pltpu.roll(lo, 7, 0), pltpu.roll(hi, 7, 0)
                        up = jnp.concatenate(
                            [jnp.where(sub == 0, 0.0, lo1), jnp.where(sub == 0, lo1, hi1)], axis=0
                        )
                        dn = jnp.concatenate(
                            [jnp.where(sub == 7, hi7, lo7), jnp.where(sub == 7, 0.0, hi7)], axis=0
                        )
                        at = vt.at[kt, 1 - o, t, 4 * g + q + o]
                        at[:, :C] = up.astype(BF16)
                        at[:, C : 2 * C] = r.astype(BF16)
                        at[:, 2 * C :] = dn.astype(BF16)

    copy_m.wait()
    for kt in range(4):

        @pl.loop(0, 3)
        def _(dh):
            @pl.loop(0, C // 16)
            def _(i):
                def tap(dt, dw):
                    at = ((dt * 3 + dh) * 3 + dw) * C + i * 16
                    return wm[pl.ds(pl.multiple_of(at, 16), 16), :]

                g = []
                for dw in range(3):
                    if kt == 0:
                        g.append(tap(0, dw))
                    elif kt == 3:
                        g.append(tap(2, dw))
                    elif kt == 1:
                        g.append((tap(0, dw) + tap(2, dw)) + tap(1, dw))
                    else:
                        g.append((tap(0, dw) + tap(2, dw)) - tap(1, dw))
                e = g[0] + g[2]
                rows = pl.ds(pl.multiple_of(dh * C + i * 16, 16), 16)
                for kc, u in enumerate((g[0], e + g[1], e - g[1], g[2])):
                    u_s[kc, rows, :] = u

        for t in range(2):

            @pl.loop(0, PAIRS)
            def _(ct):
                d0, d1 = vt[kt, 0, t, ct], vt[kt, 1, t, ct]
                d2, d3 = vt[kt, 0, t, ct + 1], vt[kt, 1, t, ct + 1]
                rows = pl.ds(pl.multiple_of((t * PAIRS + ct) * H, H), H)
                for kc, r in enumerate((d0 - d2, d1 + d2, d2 - d1, d1 - d3)):
                    v_s[kc, rows, :] = r

        for kc in range(4):
            m_s[kc] = jnp.dot(v_s[kc], u_s[kc], preferred_element_type=F32)

        @pl.loop(0, 2 * PAIRS)
        def _(i):
            rows = pl.ds(pl.multiple_of(i * H, H), H)
            m0, m1, m2, m3 = (m_s[kc, rows, :] for kc in range(4))
            y_s[kt, 0, rows, :] = m0 + 0.5 * (m1 + m2)
            y_s[kt, 1, rows, :] = 0.5 * (m1 - m2) - m3

    b_mid = bmid_ref[...].reshape(1, C)
    b_time = btime_ref[...].reshape(1, 2 * C)
    for t in range(2):

        @pl.loop(0, PAIRS)
        def _(ct):
            rows = pl.ds(pl.multiple_of((t * PAIRS + ct) * H, H), H)
            for o in range(2):
                y0, y1, y2, y3 = (y_s[kt, o, rows, :] for kt in range(4))
                for s, z in enumerate((y0 + (y1 + y2), (y1 - y2) - y3)):
                    f = 2 * t + s
                    h1 = h0_s[f, o, ct].astype(F32) + (z + b_mid)
                    h1 = h1 * jnp.where(first - 2 + f >= 0, 1.0, 0.0).astype(F32)
                    for k in range(3):
                        tr[f, k, pl.ds(2 * ct + o, H, stride=W), :] = h1[
                            :, k * 128 : (k + 1) * 128
                        ]

    for f in range(MIDF):
        for k in range(3):
            hcat[:, f * C + k * 128 : f * C + (k + 1) * 128] = tr[f, k].astype(BF16)
    copy_t.wait()
    for f in range(NT):
        up = jnp.dot(hcat[:, f * C : f * C + K3], wt[...], preferred_element_type=F32) + b_time
        for s in range(2):
            out_ref[2 * f + s] = up[:, s * C : (s + 1) * C].astype(BF16)


def per_device(latent, w_in, b_in, gain, w_mid, b_mid, w_time, b_time):
    n = lax.axis_size("tm")
    frames, width = latent.shape
    padded = jnp.concatenate([jnp.zeros((6, width), BF16), latent], axis=0)
    sent = jnp.concatenate(
        [padded[k : k + frames].reshape(n, NT, width) for k in range(0, LATF, NT)], axis=1
    )
    got = lax.all_to_all(sent, "tm", split_axis=0, concat_axis=0, tiled=True)
    x = got.transpose(1, 0, 2).reshape(LATF * H, W * ZC)
    x = jnp.pad(x, ((0, 0), (ZC, LANES - W * ZC - ZC)))
    vmem = pl.BlockSpec(memory_space=pltpu.VMEM)
    hbm = pl.BlockSpec(memory_space=pl.ANY)
    out = pl.pallas_call(
        kernel,
        out_shape=jax.ShapeDtypeStruct((2 * NT, H * W, C), BF16),
        in_specs=[vmem, vmem, vmem, vmem, hbm, vmem, hbm, vmem],
        out_specs=vmem,
        scratch_shapes=[
            pltpu.VMEM((27 * C, C), BF16),
            pltpu.VMEM((K3, 2 * C), BF16),
            pltpu.VMEM((2 * C, 2 * C), BF16),
            pltpu.VMEM((4, 4 * ACTF * H, 2 * C), BF16),
            pltpu.VMEM((MIDF, 2, PAIRS, H, C), BF16),
            pltpu.VMEM((4, 2, 2, PAIRS + 1, H, K3), BF16),
            pltpu.VMEM((4, 2 * PAIRS * H, K3), BF16),
            pltpu.VMEM((4, K3, C), BF16),
            pltpu.VMEM((4, H * W, C), F32),
            pltpu.VMEM((4, 2, 2 * PAIRS * H, C), F32),
            pltpu.VMEM((MIDF, 3, H * W, 128), F32),
            pltpu.VMEM((H * W, MIDF * C), BF16),
            pltpu.SemaphoreType.DMA,
            pltpu.SemaphoreType.DMA,
        ],
        compiler_params=pltpu.CompilerParams(vmem_limit_bytes=60 * 2**20),
    )(
        x, w_in.reshape(27 * ZC, C), b_in, gain, w_mid.reshape(27 * C, C), b_mid,
        w_time.reshape(K3, 2 * C), b_time,
    )
    return out.reshape(2 * NT, H, W, C)


def solution(mesh):
    return jax.shard_map(
        per_device,
        mesh=mesh,
        in_specs=(P("groups", "tm"), P(), P(), P(), P(), P(), P(), P()),
        out_specs=P(("groups", "tm"), None, None, None),
        check_vma=False,
    )
```

time: 155 us -> 52.5 us (0.34)
  the two profiles are of different devices: /device:TPU:10 before, /device:TPU:0 now
where the time goes in v1:
time: 52.5 us; the launch traced here: 52.1 us
  Pallas kernels  34.3 us (65%)
  blocking collectives  15.1 us (29%)
  local copies, waits for them, and re-layouts  2.55 us (5%)
    pallas_call x1, Pallas kernels, per_device(): pl.pallas_call(kernel, out_shape=jax.ShapeDtypeStruct((2 * NT, H * W, C),...  34.3 us
    all_to_all x1, blocking collectives, per_device(): got = lax.all_to_all(sent, 'tm', split_axis=0, concat_axis=0, tiled=True)  15.1 us

profile of v1, /device:TPU:0, one launch (start us, length us, event | category | flops | bytes accessed | tf_op | source)
XLA Modules:
  0.0 52.1 jit_solution(8017709106660216115)
XLA Ops:
  0.0 0.8 %reshape.30 = bf16[16,2,512]{2,1,0:T(2,128)(2,1)S(1)} reshape(bf16[32,512]{1,0:T(8,128)(2,1)} %param.8) | data formatting | bytes 65536 | tf_op jit(solution)/shard_map/reshape | solution.py:185
  0.8 0.9 %pad_slice_fusion.2 = (bf16[32,512]{1,0:T(8,128)(2,1)S(1)}, bf16[32,512]{1,0:T(8,128)(2,1)S(1)}, bf16[32,512]{1,0:T(8,128)(2,1)S(1)}) fusion(bf16[32,512]{1,0:T(8,128)(2,1)} %param.8), kind=kLoop, calls=%fused_computation.3 | loop fusion | bytes 131072 | tf_op jit(solution)/shard_map/slice | solution.py:185
  1.8 0.2 pad_maximum_fusion
  1.9 15.1 %all_to_all.5 = bf16[16,8,512]{2,1,0:T(8,128)(2,1)S(1)} all-to-all(bf16[16,8,512]{2,1,0:T(8,128)(2,1)S(1)} %pad_maximum_fusion), channel_id=1, replica_groups=mesh['groups'=2,'tm'=16] {'tm'}, dimensions={0} | all-to-all | bytes 262144 | tf_op jit(solution)/shard_map/all_to_all | solution.py:187
  17.1 0.8 %pad.5.x_ref = bf16[128,640]{1,0:T(8,128)(2,1)} pad(bf16[128,512]{1,0:T(8,128)(2,1)S(1)} %bitcast.8, bf16[]{:T(256)} %constant.1.clone.1), padding=0_0x16_112 | pad | bytes 294914 | tf_op jit(solution)/shard_map/jit(_pad)/pad | solution.py:189
  17.9 34.3 %shard_map.82 = bf16[4,512,384]{2,1,0:T(8,128)(2,1)} custom-call(bf16[128,640]{1,0:T(8,128)(2,1)} %pad.5.x_ref, bf16[432,384]{1,0:T(8,128)(2,1)} %bitcast.10, f32[384]{0:T(512)} %bin_ref.1, f32[384]{0:T(512)} %gain_ref.1, bf16[10368,384]{1,0:T(8,128)(2,1)} %bitcast.6, f32[384]{0:T(512)} %bmid_ref.1, bf16[1152,768]{1,0:T(8,128)(2,1)} %bitcast.7, f32[768]{0:T(1024)} %btime_ref.1), custom_call_target="tpu_custom_call" | custom-call | tf_op jit(solution)/shard_map/pallas_call | solution.py:192
  (4 shorter events, 0.1 us)

commit v2 on v1

--- a/solution.py
+++ b/solution.py
@@ -16,19 +16,26 @@
 PAIRS = W // 2
 LANES = 640
 K3 = 3 * C
+BLOCK = 4 * ACTF * H
+EIGHTH = C // 8
 F32 = jnp.float32
 BF16 = jnp.bfloat16
 
 
 def kernel(
     x_ref, win_ref, bin_ref, gain_ref, wm_hbm, bmid_ref, wt_hbm, btime_ref, out_ref,
-    wm, wt, toep, lhs, h0_s, vt, v_s, u_s, m_s, y_s, tr, hcat, sem_m, sem_t,
+    wm, wt, toep, lhs, h0_s, vt, v_s, u_s, m_s, y_s, hcat, perm, sem_m, sem_t,
 ):
     copy_m = pltpu.make_async_copy(wm_hbm, wm, sem_m)
     copy_t = pltpu.make_async_copy(wt_hbm, wt, sem_t)
     copy_m.start()
     copy_t.start()
     first = lax.axis_index("tm") * NT
+
+    to = lax.broadcasted_iota(jnp.int32, perm.shape, 0)
+    of = lax.broadcasted_iota(jnp.int32, perm.shape, 1)
+    source = (to % 2) * (PAIRS * H) + (to % W) // 2 * H + to // W
+    perm[...] = jnp.where(source == of, 1.0, 0.0).astype(BF16)
 
     toep[...] = jnp.zeros_like(toep)
     for dt in range(3):
@@ -58,10 +65,10 @@
         last = a2.astype(BF16)
         for g in range(4):
             for dt in range(3):
-                rows = slice(g * ACTF * H, (g + 1) * ACTF * H)
+                rows = slice(q * BLOCK + g * ACTF * H, q * BLOCK + (g + 1) * ACTF * H)
                 src = slice(dt * H, dt * H + ACTF * H)
-                lhs[q, rows, dt * 128 : dt * 128 + 128] = pair[src, g * 128 : (g + 1) * 128]
-                lhs[q, rows, 384 + dt * 128 : 512 + dt * 128] = last[src, g * 128 : (g + 1) * 128]
+                lhs[rows, dt * 128 : dt * 128 + 128] = pair[src, g * 128 : (g + 1) * 128]
+                lhs[rows, 384 + dt * 128 : 512 + dt * 128] = last[src, g * 128 : (g + 1) * 128]
 
     for kt in range(4):
         for t in range(2):
@@ -72,12 +79,16 @@
     sub = lax.broadcasted_iota(jnp.int32, (8, C), 0)
     keep = [jnp.where(first - 4 + f >= 0, 1.0, 0.0).astype(F32) for f in range(ACTF)]
 
-    @pl.loop(0, 4)
-    def _(q):
-        y = jnp.dot(lhs[q], toep[...], preferred_element_type=F32)
+    def conv_in(q, slot):
+        rows = pl.ds(pl.multiple_of(q * BLOCK, BLOCK), BLOCK)
+        y = jnp.dot(lhs[rows, :], toep[...], preferred_element_type=F32)
+        for o in range(2):
+            m_s[slot, o, :BLOCK, :] = y[:, o * C : (o + 1) * C]
+
+    def activate(q, slot):
         for o in range(2):
             for g in range(4):
-                part = y[g * ACTF * H : (g + 1) * ACTF * H, o * C : (o + 1) * C] + b_in
+                part = m_s[slot, o, g * ACTF * H : (g + 1) * ACTF * H, :] + b_in
                 hb = part.astype(BF16)
                 for f in range(2, ACTF):
                     h0_s[f - 2, o, 4 * g + q] = hb[f * H : (f + 1) * H]
@@ -103,16 +114,24 @@
                         at[:, C : 2 * C] = r.astype(BF16)
                         at[:, 2 * C :] = dn.astype(BF16)
 
+    conv_in(0, 0)
+
+    @pl.loop(0, 3)
+    def _(q):
+        conv_in(q + 1, (q + 1) % 2)
+        activate(q, q % 2)
+
+    activate(3, 1)
     copy_m.wait()
-    for kt in range(4):
-
-        @pl.loop(0, 3)
-        def _(dh):
-            @pl.loop(0, C // 16)
-            def _(i):
+
+    def weights(kt, j):
+        slot = kt % 2
+        for dh in range(3):
+            for i in range(EIGHTH // 16):
+
                 def tap(dt, dw):
-                    at = ((dt * 3 + dh) * 3 + dw) * C + i * 16
-                    return wm[pl.ds(pl.multiple_of(at, 16), 16), :]
+                    at = ((dt * 3 + dh) * 3 + dw) * C + j * EIGHTH + i * 16
+                    return wm[pl.ds(at, 16), :]
 
                 g = []
                 for dw in range(3):
@@ -125,29 +144,46 @@
                     else:
                         g.append((tap(0, dw) + tap(2, dw)) - tap(1, dw))
                 e = g[0] + g[2]
-                rows = pl.ds(pl.multiple_of(dh * C + i * 16, 16), 16)
+                rows = pl.ds(dh * C + j * EIGHTH + i * 16, 16)
                 for kc, u in enumerate((g[0], e + g[1], e - g[1], g[2])):
-                    u_s[kc, rows, :] = u
-
-        for t in range(2):
-
-            @pl.loop(0, PAIRS)
-            def _(ct):
-                d0, d1 = vt[kt, 0, t, ct], vt[kt, 1, t, ct]
-                d2, d3 = vt[kt, 0, t, ct + 1], vt[kt, 1, t, ct + 1]
-                rows = pl.ds(pl.multiple_of((t * PAIRS + ct) * H, H), H)
-                for kc, r in enumerate((d0 - d2, d1 + d2, d2 - d1, d1 - d3)):
-                    v_s[kc, rows, :] = r
-
-        for kc in range(4):
-            m_s[kc] = jnp.dot(v_s[kc], u_s[kc], preferred_element_type=F32)
-
-        @pl.loop(0, 2 * PAIRS)
-        def _(i):
-            rows = pl.ds(pl.multiple_of(i * H, H), H)
-            m0, m1, m2, m3 = (m_s[kc, rows, :] for kc in range(4))
-            y_s[kt, 0, rows, :] = m0 + 0.5 * (m1 + m2)
-            y_s[kt, 1, rows, :] = 0.5 * (m1 - m2) - m3
+                    u_s[slot, kc, rows, :] = u
+
+    def columns(kt, j):
+        slot = kt % 2
+        for i in range(4):
+            t, ct = j // 4, (j % 4) * 4 + i
+            d0, d1 = vt[kt, 0, t, ct], vt[kt, 1, t, ct]
+            d2, d3 = vt[kt, 0, t, ct + 1], vt[kt, 1, t, ct + 1]
+            rows = pl.ds((j * 4 + i) * H, H)
+            for kc, r in enumerate((d0 - d2, d1 + d2, d2 - d1, d1 - d3)):
+                v_s[slot, kc, rows, :] = r
+
+    def product(kt, j):
+        slot = kt % 2
+        kc = j // 2
+        rows = pl.ds(j % 2 * 256, 256)
+        m_s[slot, kc, rows, :] = jnp.dot(
+            v_s[slot, kc, rows, :], u_s[slot, kc], preferred_element_type=F32
+        )
+
+    def inverse(kt, rows):
+        m0, m1, m2, m3 = (m_s[kt % 2, kc, rows, :] for kc in range(4))
+        return m0 + 0.5 * (m1 + m2), 0.5 * (m1 - m2) - m3
+
+    for j in range(8):
+        weights(0, j)
+        columns(0, j)
+
+    for kt in range(4):
+        for j in range(8):
+            product(kt, j)
+            if kt < 3:
+                weights(kt + 1, j)
+                columns(kt + 1, j)
+            if kt > 0:
+                for i in range(4):
+                    rows = pl.ds((j * 4 + i) * H, H)
+                    y_s[kt - 1, 0, rows, :], y_s[kt - 1, 1, rows, :] = inverse(kt - 1, rows)
 
     b_mid = bmid_ref[...].reshape(1, C)
     b_time = btime_ref[...].reshape(1, 2 * C)
@@ -156,20 +192,20 @@
         @pl.loop(0, PAIRS)
         def _(ct):
             rows = pl.ds(pl.multiple_of((t * PAIRS + ct) * H, H), H)
+            y3s = inverse(3, rows)
             for o in range(2):
-                y0, y1, y2, y3 = (y_s[kt, o, rows, :] for kt in range(4))
+                y0, y1, y2 = (y_s[kt, o, rows, :] for kt in range(3))
+                y3 = y3s[o]
                 for s, z in enumerate((y0 + (y1 + y2), (y1 - y2) - y3)):
-                    f = 2 * t + s
-                    h1 = h0_s[f, o, ct].astype(F32) + (z + b_mid)
-                    h1 = h1 * jnp.where(first - 2 + f >= 0, 1.0, 0.0).astype(F32)
-                    for k in range(3):
-                        tr[f, k, pl.ds(2 * ct + o, H, stride=W), :] = h1[
-                            :, k * 128 : (k + 1) * 128
-                        ]
-
-    for f in range(MIDF):
-        for k in range(3):
-            hcat[:, f * C + k * 128 : f * C + (k + 1) * 128] = tr[f, k].astype(BF16)
+                    h1 = h0_s[2 * t + s, o, ct].astype(F32) + (z + b_mid)
+                    h1 = h1 * jnp.where(first - 2 + 2 * t + s >= 0, 1.0, 0.0).astype(F32)
+                    at = pl.ds(pl.multiple_of(t * H * W + o * PAIRS * H + ct * H, H), H)
+                    lhs[at, s * C : (s + 1) * C] = h1.astype(BF16)
+
+    for t in range(2):
+        hcat[:, 2 * t * C : 2 * (t + 1) * C] = jnp.dot(
+            perm[...], lhs[t * H * W : (t + 1) * H * W, :], preferred_element_type=F32
+        ).astype(BF16)
     copy_t.wait()
     for f in range(NT):
         up = jnp.dot(hcat[:, f * C : f * C + K3], wt[...], preferred_element_type=F32) + b_time
@@ -198,19 +234,19 @@
             pltpu.VMEM((27 * C, C), BF16),
             pltpu.VMEM((K3, 2 * C), BF16),
             pltpu.VMEM((2 * C, 2 * C), BF16),
-            pltpu.VMEM((4, 4 * ACTF * H, 2 * C), BF16),
+            pltpu.VMEM((4 * BLOCK, 2 * C), BF16),
             pltpu.VMEM((MIDF, 2, PAIRS, H, C), BF16),
             pltpu.VMEM((4, 2, 2, PAIRS + 1, H, K3), BF16),
-            pltpu.VMEM((4, 2 * PAIRS * H, K3), BF16),
-            pltpu.VMEM((4, K3, C), BF16),
-            pltpu.VMEM((4, H * W, C), F32),
-            pltpu.VMEM((4, 2, 2 * PAIRS * H, C), F32),
-            pltpu.VMEM((MIDF, 3, H * W, 128), F32),
+            pltpu.VMEM((2, 4, 2 * PAIRS * H, K3), BF16),
+            pltpu.VMEM((2, 4, K3, C), BF16),
+            pltpu.VMEM((2, 4, H * W, C), F32),
+            pltpu.VMEM((3, 2, 2 * PAIRS * H, C), F32),
             pltpu.VMEM((H * W, MIDF * C), BF16),
+            pltpu.VMEM((H * W, H * W), BF16),
             pltpu.SemaphoreType.DMA,
             pltpu.SemaphoreType.DMA,
         ],
-        compiler_params=pltpu.CompilerParams(vmem_limit_bytes=60 * 2**20),
+        compiler_params=pltpu.CompilerParams(vmem_limit_bytes=62 * 2**20),
     )(
         x, w_in.reshape(27 * ZC, C), b_in, gain, w_mid.reshape(27 * C, C), b_mid,
         w_time.reshape(K3, 2 * C), b_time,

time: 52.5 us -> 44.5 us (0.85)
  Pallas kernels: 34.3 us -> 26.2 us
    pallas_call x1, Pallas kernels: 34.3 us -> 26.2 us  [per_device(): pl.pallas_call(kernel, out_shape=jax.ShapeDtypeStruct((2 * NT, H * W, C),...]
where the time goes in v2:
time: 44.5 us; the launch traced here: 44.2 us
  Pallas kernels  26.2 us (59%)
  blocking collectives  15.1 us (34%)
  local copies, waits for them, and re-layouts  2.55 us (6%)
    pallas_call x1, Pallas kernels, per_device(): pl.pallas_call(kernel, out_shape=jax.ShapeDtypeStruct((2 * NT, H * W, C),...  26.2 us
    all_to_all x1, blocking collectives, per_device(): got = lax.all_to_all(sent, 'tm', split_axis=0, concat_axis=0, tiled=True)  15.1 us
    slice x1, local copies, waits for them, and re-layouts, per_device(): padded[k:k + frames].reshape(n, NT, width)  0.9 us

profile of v2, /device:TPU:0, one launch (start us, length us, event | category | flops | bytes accessed | tf_op | source)
XLA Modules:
  0.0 44.2 jit_solution(2110853319027904907)
XLA Ops:
  0.0 0.8 %reshape.30 = bf16[16,2,512]{2,1,0:T(2,128)(2,1)S(1)} reshape(bf16[32,512]{1,0:T(8,128)(2,1)} %param.8) | data formatting | bytes 65536 | tf_op jit(solution)/shard_map/reshape | solution.py:221
  0.8 0.9 %pad_slice_fusion.2 = (bf16[32,512]{1,0:T(8,128)(2,1)S(1)}, bf16[32,512]{1,0:T(8,128)(2,1)S(1)}, bf16[32,512]{1,0:T(8,128)(2,1)S(1)}) fusion(bf16[32,512]{1,0:T(8,128)(2,1)} %param.8), kind=kLoop, calls=%fused_computation.3 | loop fusion | bytes 131072 | tf_op jit(solution)/shard_map/slice | solution.py:221
  1.8 0.2 pad_maximum_fusion
  1.9 15.1 %all_to_all.5 = bf16[16,8,512]{2,1,0:T(8,128)(2,1)S(1)} all-to-all(bf16[16,8,512]{2,1,0:T(8,128)(2,1)S(1)} %pad_maximum_fusion), channel_id=1, replica_groups=mesh['groups'=2,'tm'=16] {'tm'}, dimensions={0} | all-to-all | bytes 262144 | tf_op jit(solution)/shard_map/all_to_all | solution.py:223
  17.1 0.8 %pad.5.x_ref = bf16[128,640]{1,0:T(8,128)(2,1)} pad(bf16[128,512]{1,0:T(8,128)(2,1)S(1)} %bitcast.8, bf16[]{:T(256)} %constant.1.clone.1), padding=0_0x16_112 | pad | bytes 294914 | tf_op jit(solution)/shard_map/jit(_pad)/pad | solution.py:225
  17.9 26.2 %shard_map.82 = bf16[4,512,384]{2,1,0:T(8,128)(2,1)} custom-call(bf16[128,640]{1,0:T(8,128)(2,1)} %pad.5.x_ref, bf16[432,384]{1,0:T(8,128)(2,1)} %bitcast.10, f32[384]{0:T(512)} %bin_ref.1, f32[384]{0:T(512)} %gain_ref.1, bf16[10368,384]{1,0:T(8,128)(2,1)} %bitcast.6, f32[384]{0:T(512)} %bmid_ref.1, bf16[1152,768]{1,0:T(8,128)(2,1)} %bitcast.7, f32[768]{0:T(1024)} %btime_ref.1), custom_call_target="tpu_custom_call" | custom-call | tf_op jit(solution)/shard_map/pallas_call | solution.py:228
  (4 shorter events, 0.1 us)

commit v3 on v2

--- a/solution.py
+++ b/solution.py
@@ -23,13 +23,16 @@
 
 
 def kernel(
-    x_ref, win_ref, bin_ref, gain_ref, wm_hbm, bmid_ref, wt_hbm, btime_ref, out_ref,
-    wm, wt, toep, lhs, h0_s, vt, v_s, u_s, m_s, y_s, hcat, perm, sem_m, sem_t,
+    x_hbm, win_hbm, bin_ref, gain_ref, wm_hbm, bmid_ref, wt_hbm, btime_ref, out_hbm,
+    x_s, win, wm, wt, toep, lhs, h0_s, vt, v_s, u_s, m_s, y_s, hcat, perm, out_s, sems, out_sems,
 ):
-    copy_m = pltpu.make_async_copy(wm_hbm, wm, sem_m)
-    copy_t = pltpu.make_async_copy(wt_hbm, wt, sem_t)
-    copy_m.start()
-    copy_t.start()
+    copies = [
+        pltpu.make_async_copy(src, dst, sems.at[i])
+        for i, (src, dst) in enumerate(((x_hbm, x_s), (win_hbm, win), (wm_hbm, wm), (wt_hbm, wt)))
+    ]
+    for copy in copies:
+        copy.start()
+    copy_x, copy_in, copy_m, copy_t = copies
     first = lax.axis_index("tm") * NT
 
     to = lax.broadcasted_iota(jnp.int32, perm.shape, 0)
@@ -38,6 +41,7 @@
     perm[...] = jnp.where(source == of, 1.0, 0.0).astype(BF16)
 
     toep[...] = jnp.zeros_like(toep)
+    copy_in.wait()
     for dt in range(3):
         for dh in range(3):
             base = dt * 128 + dh * 64 if dh < 2 else 384 + dt * 128
@@ -46,11 +50,24 @@
                     dw = j - o
                     if 0 <= dw <= 2:
                         tap = ((dt * 3 + dh) * 3 + dw) * ZC
-                        toep[base + 16 * j : base + 16 * j + 16, o * C : (o + 1) * C] = win_ref[
+                        toep[base + 16 * j : base + 16 * j + 16, o * C : (o + 1) * C] = win[
                             tap : tap + ZC, :
                         ]
 
-    x = x_ref[...].astype(F32)
+    copy_x.wait()
+    pieces = W * ZC // x_s.shape[1]
+    to = lax.broadcasted_iota(jnp.int32, (LATF * H, x_s.shape[0]), 0)
+    of = lax.broadcasted_iota(jnp.int32, (LATF * H, x_s.shape[0]), 1)
+    x = [
+        jnp.dot(
+            jnp.where((to % H * pieces + i) * LATF + to // H == of, 1.0, 0.0).astype(BF16),
+            x_s[...],
+            preferred_element_type=F32,
+        )
+        for i in range(pieces)
+    ]
+    x = jnp.concatenate([*x, jnp.zeros((LATF * H, LANES - W * ZC), F32)], axis=1)
+    x = pltpu.roll(x, ZC, 1)
     row = lax.broadcasted_iota(jnp.int32, x.shape, 0) % H
     lane = lax.broadcasted_iota(jnp.int32, x.shape, 1) % 128
     above = jnp.where(row == 0, 0.0, pltpu.roll(x, 1, 0))
@@ -75,9 +92,10 @@
             vt[kt, 0, t, 0] = jnp.zeros((H, K3), BF16)
             vt[kt, 1, t, PAIRS] = jnp.zeros((H, K3), BF16)
     b_in = bin_ref[...].reshape(1, C)
-    gain = gain_ref[...].reshape(1, C)
+    half_gain = 0.5 * gain_ref[...].reshape(1, C)
     sub = lax.broadcasted_iota(jnp.int32, (8, C), 0)
-    keep = [jnp.where(first - 4 + f >= 0, 1.0, 0.0).astype(F32) for f in range(ACTF)]
+    frame = lax.broadcasted_iota(jnp.int32, (ACTF * H, 1), 0) // H + (first - 4)
+    keep = jnp.where(frame >= 0, 1.0, 0.0).astype(F32)
 
     def conv_in(q, slot):
         rows = pl.ds(pl.multiple_of(q * BLOCK, BLOCK), BLOCK)
@@ -94,9 +112,9 @@
                     h0_s[f - 2, o, 4 * g + q] = hb[f * H : (f + 1) * H]
                 h = hb.astype(F32)
                 scale = lax.rsqrt(jnp.mean(h * h, axis=-1, keepdims=True) + 1e-06)
-                v = h * scale * gain
-                a = 0.5 * v * (1.0 + jnp.tanh(0.5 * v))
-                d = [a[f * H : (f + 1) * H] * keep[f] for f in range(ACTF)]
+                v = h * (scale * keep) * half_gain
+                a = v + v * jnp.tanh(v)
+                d = [a[f * H : (f + 1) * H] for f in range(ACTF)]
                 for t in range(2):
                     d0, d1, d2, d3 = d[2 * t : 2 * t + 4]
                     for kt, r in enumerate((d0 - d2, 0.5 * (d1 + d2), 0.5 * (d2 - d1), d1 - d3)):
@@ -188,49 +206,64 @@
     b_mid = bmid_ref[...].reshape(1, C)
     b_time = btime_ref[...].reshape(1, 2 * C)
     for t in range(2):
-
-        @pl.loop(0, PAIRS)
-        def _(ct):
-            rows = pl.ds(pl.multiple_of((t * PAIRS + ct) * H, H), H)
+        for ct in range(PAIRS):
+            rows = slice((t * PAIRS + ct) * H, (t * PAIRS + ct + 1) * H)
             y3s = inverse(3, rows)
             for o in range(2):
                 y0, y1, y2 = (y_s[kt, o, rows, :] for kt in range(3))
                 y3 = y3s[o]
                 for s, z in enumerate((y0 + (y1 + y2), (y1 - y2) - y3)):
                     h1 = h0_s[2 * t + s, o, ct].astype(F32) + (z + b_mid)
-                    h1 = h1 * jnp.where(first - 2 + 2 * t + s >= 0, 1.0, 0.0).astype(F32)
-                    at = pl.ds(pl.multiple_of(t * H * W + o * PAIRS * H + ct * H, H), H)
-                    lhs[at, s * C : (s + 1) * C] = h1.astype(BF16)
-
-    for t in range(2):
+                    if t == 0:
+                        h1 = h1 * jnp.where(first - 2 + s >= 0, 1.0, 0.0).astype(F32)
+                    at = t * H * W + o * PAIRS * H + ct * H
+                    lhs[at : at + H, s * C : (s + 1) * C] = h1.astype(BF16)
         hcat[:, 2 * t * C : 2 * (t + 1) * C] = jnp.dot(
             perm[...], lhs[t * H * W : (t + 1) * H * W, :], preferred_element_type=F32
         ).astype(BF16)
     copy_t.wait()
+    sent = []
     for f in range(NT):
-        up = jnp.dot(hcat[:, f * C : f * C + K3], wt[...], preferred_element_type=F32) + b_time
-        for s in range(2):
-            out_ref[2 * f + s] = up[:, s * C : (s + 1) * C].astype(BF16)
+        for part in range(2):
+            rows = slice(part * H * W // 2, (part + 1) * H * W // 2)
+            up = jnp.dot(hcat[rows, f * C : f * C + K3], wt[...], preferred_element_type=F32) + b_time
+            for s in range(2):
+                out_s[2 * f + s, rows, :] = up[:, s * C : (s + 1) * C].astype(BF16)
+            here = (slice(2 * f, 2 * f + 2), rows)
+            copy = pltpu.make_async_copy(out_s.at[here], out_hbm.at[here], out_sems.at[f, part])
+            copy.start()
+            sent.append(copy)
+    for copy in sent:
+        copy.wait()
+
+
+def pack(latent_ref, out_ref, held):
+    held[:LATF] = jnp.zeros_like(held[:LATF])
+    held[LATF:] = latent_ref[...].astype(F32)
+    for i in range(out_ref.shape[0]):
+        out_ref[i] = held[NT * (i + 1) : NT * (i + 1) + LATF].astype(BF16)
 
 
 def per_device(latent, w_in, b_in, gain, w_mid, b_mid, w_time, b_time):
     n = lax.axis_size("tm")
     frames, width = latent.shape
-    padded = jnp.concatenate([jnp.zeros((6, width), BF16), latent], axis=0)
-    sent = jnp.concatenate(
-        [padded[k : k + frames].reshape(n, NT, width) for k in range(0, LATF, NT)], axis=1
-    )
-    got = lax.all_to_all(sent, "tm", split_axis=0, concat_axis=0, tiled=True)
-    x = got.transpose(1, 0, 2).reshape(LATF * H, W * ZC)
-    x = jnp.pad(x, ((0, 0), (ZC, LANES - W * ZC - ZC)))
+    sent = pl.pallas_call(
+        pack,
+        out_shape=jax.ShapeDtypeStruct((n, LATF, width), BF16),
+        scratch_shapes=[pltpu.VMEM((LATF + frames, width), F32)],
+    )(latent)
+    x = lax.all_to_all(sent, "tm", split_axis=0, concat_axis=0, tiled=True)
+    x = x.reshape(n * LATF, width)
     vmem = pl.BlockSpec(memory_space=pltpu.VMEM)
     hbm = pl.BlockSpec(memory_space=pl.ANY)
     out = pl.pallas_call(
         kernel,
         out_shape=jax.ShapeDtypeStruct((2 * NT, H * W, C), BF16),
-        in_specs=[vmem, vmem, vmem, vmem, hbm, vmem, hbm, vmem],
-        out_specs=vmem,
+        in_specs=[hbm, hbm, vmem, vmem, hbm, vmem, hbm, vmem],
+        out_specs=hbm,
         scratch_shapes=[
+            pltpu.VMEM((n * LATF, width), BF16),
+            pltpu.VMEM((27 * ZC, C), BF16),
             pltpu.VMEM((27 * C, C), BF16),
             pltpu.VMEM((K3, 2 * C), BF16),
             pltpu.VMEM((2 * C, 2 * C), BF16),
@@ -243,10 +276,11 @@
             pltpu.VMEM((3, 2, 2 * PAIRS * H, C), F32),
             pltpu.VMEM((H * W, MIDF * C), BF16),
             pltpu.VMEM((H * W, H * W), BF16),
-            pltpu.SemaphoreType.DMA,
-            pltpu.SemaphoreType.DMA,
+            pltpu.VMEM((2 * NT, H * W, C), BF16),
+            pltpu.SemaphoreType.DMA((4,)),
+            pltpu.SemaphoreType.DMA((NT, 2)),
         ],
-        compiler_params=pltpu.CompilerParams(vmem_limit_bytes=62 * 2**20),
+        compiler_params=pltpu.CompilerParams(vmem_limit_bytes=61 * 2**20),
     )(
         x, w_in.reshape(27 * ZC, C), b_in, gain, w_mid.reshape(27 * C, C), b_mid,
         w_time.reshape(K3, 2 * C), b_time,

time: 44.5 us -> 42.6 us (0.957)
  local copies, waits for them, and re-layouts: 2.55 us -> 0 us
  Pallas kernels: 26.2 us -> 26.7 us
    pallas_call x0 -> x1, Pallas kernels: none -> 1.45 us  [per_device(): pl.pallas_call(pack, out_shape=jax.ShapeDtypeStruct((n, LATF, width), BF1...]
    pallas_call x1, Pallas kernels: 26.2 us -> 25.2 us  [per_device(): pl.pallas_call(kernel, out_shape=jax.ShapeDtypeStruct((2 * NT, H * W, C),...]
    slice x1 -> x0, local copies, waits for them, and re-layouts: 0.9 us -> none  [per_device(): padded[k:k + frames].reshape(n, NT, width)]
    reshape x4 -> x0, local copies, waits for them, and re-layouts: 0.83 us -> none  [per_device(): padded[k:k + frames].reshape(n, NT, width)]
    pad x1 -> x0, local copies, waits for them, and re-layouts: 0.78 us -> none  [per_device(): x = jnp.pad(x, ((0, 0), (ZC, LANES - W * ZC - ZC)))]
where the time goes in v3:
time: 42.6 us; the launch traced here: 42.3 us
  Pallas kernels  26.7 us (63%)
  blocking collectives  15.4 us (36%)
    pallas_call x1, Pallas kernels, per_device(): pl.pallas_call(kernel, out_shape=jax.ShapeDtypeStruct((2 * NT, H * W, C),...  25.2 us
    all_to_all x1, blocking collectives, per_device(): x = lax.all_to_all(sent, 'tm', split_axis=0, concat_axis=0, tiled=True)  15.4 us
    pallas_call x1, Pallas kernels, per_device(): pl.pallas_call(pack, out_shape=jax.ShapeDtypeStruct((n, LATF, width), BF1...  1.45 us

profile of v3, /device:TPU:0, one launch (start us, length us, event | category | flops | bytes accessed | tf_op | source)
XLA Modules:
  0.0 42.3 jit_solution(3952134621005743192)
XLA Ops:
  0.0 1.4 %shard_map.82 = bf16[16,8,512]{2,1,0:T(8,128)(2,1)} custom-call(bf16[32,512]{1,0:T(8,128)(2,1)} %latent_ref.1), custom_call_target="tpu_custom_call" | custom-call | tf_op jit(solution)/shard_map/pallas_call | solution.py:250
  1.4 15.4 %all_to_all.5 = bf16[16,8,512]{2,1,0:T(8,128)(2,1)} all-to-all(bf16[16,8,512]{2,1,0:T(8,128)(2,1)} %shard_map.82), channel_id=1, replica_groups=mesh['groups'=2,'tm'=16] {'tm'}, dimensions={0} | all-to-all | bytes 262144 | tf_op jit(solution)/shard_map/all_to_all | solution.py:255
  16.9 25.2 %shard_map.83 = bf16[4,512,384]{2,1,0:T(8,128)(2,1)} custom-call(bf16[128,512]{1,0:T(8,128)(2,1)} %bitcast.7, bf16[432,384]{1,0:T(8,128)(2,1)} %bitcast.8, f32[384]{0:T(512)} %bin_ref.1, f32[384]{0:T(512)} %gain_ref.1, bf16[10368,384]{1,0:T(8,128)(2,1)} %bitcast.5, f32[384]{0:T(512)} %bmid_ref.1, bf16[1152,768]{1,0:T(8,128)(2,1)} %bitcast.6, f32[768]{0:T(1024)} %btime_ref.1), custom_call_target="tpu_custom_call" | custom-call | tf_op jit(solution)/shard_map/pallas_call | solution.py:259

commit v4 on v3

v4 whole, which is shorter than its diff:
```python
import functools

import jax
import jax.numpy as jnp
from jax import lax
from jax.experimental import pallas as pl
from jax.experimental.pallas import tpu as pltpu
from jax.sharding import PartitionSpec as P

ZC = 16
C = 384
H = 16
W = 32
NT = 2
LATF = NT + 6
ACTF = NT + 4
MIDF = NT + 2
PAIRS = W // 2
LANES = 640
K3 = 3 * C
BLOCK = 4 * ACTF * H
POINTS = 6
ORDER = (0, 5, 1, 2, 3, 4)
QUARTER = C // 4
EIGHTH = C // 8
F32 = jnp.float32
BF16 = jnp.bfloat16


def time_points(d0, d1, d2, d3, d4, d5):
    p, q = d3 - d1, d4 - d2
    a, b = q + 1.5 * d3, p + 1.5 * d2
    first = (d0 - d2) + (q + 1.5 * p)
    last = (d5 - d3) + (1.5 * q - p)
    return first, a + b, a - b, 2.0 * p + q, 2.0 * q - p, last


def time_weights(kt, dw, tap):
    if kt == 0:
        return tap(0, dw)
    if kt == 5:
        return tap(2, dw)
    g0, g1, g2 = (tap(dt, dw) for dt in range(3))
    if kt == 1:
        return (g0 + g2) + g1
    if kt == 2:
        return (g0 + g2) - g1
    if kt == 3:
        return (4.0 * g0 + g2) + 2.0 * g1
    return (g0 + 4.0 * g2) - 2.0 * g1


def time_frames(m0, m1, m2, m3, m4, m5):
    s, d = (m1 - m2) * (1 / 3), (m1 + m2) * (1 / 3)
    a, b = m3 * (-4 / 15), m4 * (1 / 30)
    return (
        (m0 + s) + (a + b),
        d + (0.5 * a - 2.0 * b),
        s + (0.25 * a + 4.0 * b),
        (d + m5) + (0.125 * a - 8.0 * b),
    )


def kernel(
    x_hbm, win_hbm, bin_ref, gain_ref, wm_hbm, bmid_ref, wt_hbm, btime_ref, out_hbm,
    x_s, win, wm, wt, toep, lhs, h1_s, h0_s, vt, v_s, u_s, m_s, y_s, hcat, perm, sems, out_sems,
):
    copies = [
        pltpu.make_async_copy(src, dst, sems.at[i])
        for i, (src, dst) in enumerate(((x_hbm, x_s), (win_hbm, win), (wm_hbm, wm), (wt_hbm, wt)))
    ]
    for copy in copies:
        copy.start()
    copy_x, copy_in, copy_m, copy_t = copies
    first = lax.axis_index("tm") * NT

    to = lax.broadcasted_iota(jnp.int32, perm.shape, 0)
    of = lax.broadcasted_iota(jnp.int32, perm.shape, 1)
    source = (to % 2) * (PAIRS * H) + (to % W) // 2 * H + to // W
    perm[...] = jnp.where(source == of, 1.0, 0.0).astype(BF16)

    toep[...] = jnp.zeros_like(toep)
    copy_in.wait()
    for dt in range(3):
        for dh in range(3):
            base = dt * 128 + dh * 64 if dh < 2 else 384 + dt * 128
            for j in range(4):
                for o in range(2):
                    dw = j - o
                    if 0 <= dw <= 2:
                        tap = ((dt * 3 + dh) * 3 + dw) * ZC
                        toep[base + 16 * j : base + 16 * j + 16, o * C : (o + 1) * C] = win[
                            tap : tap + ZC, :
                        ]

    copy_x.wait()
    pieces = W * ZC // x_s.shape[1]
    to = lax.broadcasted_iota(jnp.int32, (LATF * H, x_s.shape[0]), 0)
    of = lax.broadcasted_iota(jnp.int32, (LATF * H, x_s.shape[0]), 1)
    x = [
        jnp.dot(
            jnp.where((to % H * pieces + i) * LATF + to // H == of, 1.0, 0.0).astype(BF16),
            x_s[...],
            preferred_element_type=F32,
        )
        for i in range(pieces)
    ]
    x = jnp.concatenate([*x, jnp.zeros((LATF * H, LANES - W * ZC), F32)], axis=1)
    x = pltpu.roll(x, ZC, 1)
    row = lax.broadcasted_iota(jnp.int32, x.shape, 0) % H
    lane = lax.broadcasted_iota(jnp.int32, x.shape, 1) % 128
    above = jnp.where(row == 0, 0.0, pltpu.roll(x, 1, 0))
    below = jnp.where(row == H - 1, 0.0, pltpu.roll(x, x.shape[0] - 1, 0))
    for q in range(4):
        left = (LANES - 32 * q) % LANES
        mid = (LANES + 64 - 32 * q) % LANES
        a0 = pltpu.roll(above, left, 1) if left else above
        a1 = pltpu.roll(x, mid, 1) if mid else x
        a2 = pltpu.roll(below, left, 1) if left else below
        pair = jnp.where(lane < 64, a0, a1).astype(BF16)
        last = a2.astype(BF16)
        for g in range(4):
            for dt in range(3):
                rows = slice(g * ACTF * H, (g + 1) * ACTF * H)
                src = slice(dt * H, dt * H + ACTF * H)
                lhs[q][rows, dt * 128 : dt * 128 + 128] = pair[src, g * 128 : (g + 1) * 128]
                lhs[q][rows, 384 + dt * 128 : 512 + dt * 128] = last[src, g * 128 : (g + 1) * 128]

    for kt in range(POINTS):
        vt[kt][0, 0] = jnp.zeros((H, K3), BF16)
        vt[kt][1, PAIRS] = jnp.zeros((H, K3), BF16)
    b_in = bin_ref[...].reshape(1, C)
    half_gain = 0.5 * gain_ref[...].reshape(1, C)
    sub = lax.broadcasted_iota(jnp.int32, (8, C), 0)
    frame = lax.broadcasted_iota(jnp.int32, (ACTF * H, 1), 0) // H + (first - 4)
    keep = jnp.where(frame >= 0, 1.0, 0.0).astype(F32)

    def conv_in(q):
        y = jnp.dot(lhs[q][...], toep[...], preferred_element_type=F32)
        for o in range(2):
            m_s[q % 2][o * BLOCK : (o + 1) * BLOCK, :] = y[:, o * C : (o + 1) * C]

    def activate(q):
        for o in range(2):
            for g in range(4):
                at = o * BLOCK + g * ACTF * H
                part = m_s[q % 2][at : at + ACTF * H, :] + b_in
                hb = part.astype(BF16)
                for f in range(2, ACTF):
                    h0_s[f - 2, o, 4 * g + q] = hb[f * H : (f + 1) * H]
                h = hb.astype(F32)
                scale = lax.rsqrt(jnp.mean(h * h, axis=-1, keepdims=True) + 1e-06)
                v = h * (scale * keep) * half_gain
                a = v + v * jnp.tanh(v)
                d = [a[f * H : (f + 1) * H] for f in range(ACTF)]
                for kt, r in enumerate(time_points(*d)):
                    lo, hi = r[:8], r[8:]
                    lo1, hi1 = pltpu.roll(lo, 1, 0), pltpu.roll(hi, 1, 0)
                    lo7, hi7 = pltpu.roll(lo, 7, 0), pltpu.roll(hi, 7, 0)
                    up = jnp.concatenate(
                        [jnp.where(sub == 0, 0.0, lo1), jnp.where(sub == 0, lo1, hi1)], axis=0
                    )
                    dn = jnp.concatenate(
                        [jnp.where(sub == 7, hi7, lo7), jnp.where(sub == 7, 0.0, hi7)], axis=0
                    )
                    at = vt[kt].at[1 - o, 4 * g + q + o]
                    at[:, :C] = up.astype(BF16)
                    at[:, C : 2 * C] = r.astype(BF16)
                    at[:, 2 * C :] = dn.astype(BF16)

    conv_in(0)
    for q in range(4):
        if q < 3:
            conv_in(q + 1)
        activate(q)
    copy_m.wait()

    def weights(kts, start, size):
        for dh in range(3):
            for i in range(start, start + size, 16):

                @functools.cache
                def tap(dt, dw):
                    at = ((dt * 3 + dh) * 3 + dw) * C + i
                    return wm[at : at + 16, :]

                for kt in kts:
                    g0, g1, g2 = (time_weights(kt, dw, tap) for dw in range(3))
                    e = g0 + g2
                    at = dh * C + i
                    for kc, u in enumerate((g0, e + g1, e - g1, g2)):
                        u_s[kt][kc, at : at + 16, :] = u

    def columns(n, j):
        kt = ORDER[n]
        for k in range(3):
            part = slice(k * C, (k + 1) * C)
            d0, d1 = vt[kt][0, j * 4, :, part], vt[kt][1, j * 4, :, part]
            for ct in range(j * 4, j * 4 + 4):
                d2, d3 = vt[kt][0, ct + 1, :, part], vt[kt][1, ct + 1, :, part]
                for kc, r in enumerate((d0 - d2, d1 + d2, d2 - d1, d1 - d3)):
                    v_s[n % 2][kc, ct * H : (ct + 1) * H, part] = r
                d0, d1 = d2, d3

    def product(n, kc):
        m_s[n % 2][kc * PAIRS * H : (kc + 1) * PAIRS * H, :] = jnp.dot(
            v_s[n % 2][kc], u_s[ORDER[n]][kc], preferred_element_type=F32
        )

    def inverse(n, ct):
        at = [(kc * PAIRS + ct) * H for kc in range(4)]
        m0, m1, m2, m3 = (m_s[n % 2][i : i + H, :] for i in at)
        return m0 + 0.5 * (m1 + m2), 0.5 * (m1 - m2) - m3

    def held(n, o, ct):
        at = ((n * 2 + o) * PAIRS + ct) * H
        return slice(at, at + H)

    weights((ORDER[0],), 0, C)
    for j in range(4):
        columns(0, j)

    for n in range(POINTS):
        for j in range(4):
            product(n, j)
            if n == 0:
                weights((ORDER[1],), j * QUARTER, QUARTER)
            if n < 2:
                weights(ORDER[2:4], (n * 4 + j) * EIGHTH, EIGHTH)
            elif n < 4:
                weights(ORDER[4:], (n * 4 + j - 8) * EIGHTH, EIGHTH)
            if n < POINTS - 1:
                columns(n + 1, j)
            if n > 0:
                for ct in range(j * 4, j * 4 + 4):
                    even, odd = inverse(n - 1, ct)
                    y_s[held(n - 1, 0, ct), :] = even
                    y_s[held(n - 1, 1, ct), :] = odd

    b_mid = bmid_ref[...].reshape(1, C)
    b_time = btime_ref[...].reshape(1, 2 * C)
    for ct in range(PAIRS):
        last = inverse(POINTS - 1, ct)
        for o in range(2):
            points = [y_s[held(n, o, ct), :] for n in range(POINTS - 1)] + [last[o]]
            points = [points[ORDER.index(kt)] for kt in range(POINTS)]
            for f, z in enumerate(time_frames(*points)):
                h1 = h0_s[f, o, ct].astype(F32) + (z + b_mid)
                if f < 2:
                    h1 = h1 * jnp.where(first - 2 + f >= 0, 1.0, 0.0).astype(F32)
                at = (o * PAIRS + ct) * H
                h1_s[f // 2][at : at + H, f % 2 * C : (f % 2 + 1) * C] = h1.astype(BF16)
    for t in range(2):
        hcat[:, 2 * t * C : 2 * (t + 1) * C] = jnp.dot(
            perm[...], h1_s[t][...], preferred_element_type=F32
        ).astype(BF16)
    copy_t.wait()
    sent = []
    for f in range(NT):
        for part in range(2):
            rows = slice(part * H * W // 2, (part + 1) * H * W // 2)
            up = jnp.dot(hcat[rows, f * C : f * C + K3], wt[...], preferred_element_type=F32) + b_time
            for s in range(2):
                u_s[0][2 * f + s, rows, :] = up[:, s * C : (s + 1) * C].astype(BF16)
            two = slice(2 * f, 2 * f + 2)
            copy = pltpu.make_async_copy(
                u_s[0].at[two, rows], out_hbm.at[two, rows], out_sems.at[f, part]
            )
            copy.start()
            sent.append(copy)
    for copy in sent:
        copy.wait()


def pack(latent_ref, out_ref, held):
    held[:LATF] = jnp.zeros_like(held[:LATF])
    held[LATF:] = latent_ref[...].astype(F32)
    for i in range(out_ref.shape[0]):
        out_ref[i] = held[NT * (i + 1) : NT * (i + 1) + LATF].astype(BF16)


def per_device(latent, w_in, b_in, gain, w_mid, b_mid, w_time, b_time):
    n = lax.axis_size("tm")
    frames, width = latent.shape
    sent = pl.pallas_call(
        pack,
        out_shape=jax.ShapeDtypeStruct((n, LATF, width), BF16),
        scratch_shapes=[pltpu.VMEM((LATF + frames, width), F32)],
    )(latent)
    x = lax.all_to_all(sent, "tm", split_axis=0, concat_axis=0, tiled=True)
    x = x.reshape(n * LATF, width)
    vmem = pl.BlockSpec(memory_space=pltpu.VMEM)
    hbm = pl.BlockSpec(memory_space=pl.ANY)
    out = pl.pallas_call(
        kernel,
        out_shape=jax.ShapeDtypeStruct((2 * NT, H * W, C), BF16),
        in_specs=[hbm, hbm, vmem, vmem, hbm, vmem, hbm, vmem],
        out_specs=hbm,
        scratch_shapes=[
            pltpu.VMEM((n * LATF, width), BF16),
            pltpu.VMEM((27 * ZC, C), BF16),
            pltpu.VMEM((27 * C, C), BF16),
            pltpu.VMEM((K3, 2 * C), BF16),
            pltpu.VMEM((2 * C, 2 * C), BF16),
            [pltpu.VMEM((BLOCK, 2 * C), BF16)] * 4,
            [pltpu.VMEM((H * W, 2 * C), BF16)] * 2,
            pltpu.VMEM((MIDF, 2, PAIRS, H, C), BF16),
            [pltpu.VMEM((2, PAIRS + 1, H, K3), BF16)] * POINTS,
            [pltpu.VMEM((4, PAIRS * H, K3), BF16)] * 2,
            [pltpu.VMEM((4, K3, C), BF16)] * POINTS,
            [pltpu.VMEM((4 * PAIRS * H, C), F32)] * 2,
            pltpu.VMEM(((POINTS - 1) * 2 * PAIRS * H, C), F32),
            pltpu.VMEM((H * W, MIDF * C), BF16),
            pltpu.VMEM((H * W, H * W), BF16),
            pltpu.SemaphoreType.DMA((4,)),
            pltpu.SemaphoreType.DMA((NT, 2)),
        ],
        compiler_params=pltpu.CompilerParams(vmem_limit_bytes=61 * 2**20),
    )(
        x, w_in.reshape(27 * ZC, C), b_in, gain, w_mid.reshape(27 * C, C), b_mid,
        w_time.reshape(K3, 2 * C), b_time,
    )
    return out.reshape(2 * NT, H, W, C)


def solution(mesh):
    return jax.shard_map(
        per_device,
        mesh=mesh,
        in_specs=(P("groups", "tm"), P(), P(), P(), P(), P(), P(), P()),
        out_specs=P(("groups", "tm"), None, None, None),
        check_vma=False,
    )
```

time: 42.6 us -> 40 us (0.939)
  Pallas kernels: 26.7 us -> 24.1 us
    pallas_call x1, Pallas kernels: 25.2 us -> 22.6 us  [per_device(): pl.pallas_call(kernel, out_shape=jax.ShapeDtypeStruct((2 * NT, H * W, C),...]
where the time goes in v4:
time: 40 us; the launch traced here: 39.7 us
  Pallas kernels  24.1 us (60%)
  blocking collectives  15.4 us (38%)
    pallas_call x1, Pallas kernels, per_device(): pl.pallas_call(kernel, out_shape=jax.ShapeDtypeStruct((2 * NT, H * W, C),...  22.6 us
    all_to_all x1, blocking collectives, per_device(): x = lax.all_to_all(sent, 'tm', split_axis=0, concat_axis=0, tiled=True)  15.4 us
    pallas_call x1, Pallas kernels, per_device(): pl.pallas_call(pack, out_shape=jax.ShapeDtypeStruct((n, LATF, width), BF1...  1.45 us

profile of v4, /device:TPU:0, one launch (start us, length us, event | category | flops | bytes accessed | tf_op | source)
XLA Modules:
  0.0 39.7 jit_solution(9755345318721206978)
XLA Ops:
  0.0 1.4 %shard_map.82 = bf16[16,8,512]{2,1,0:T(8,128)(2,1)} custom-call(bf16[32,512]{1,0:T(8,128)(2,1)} %latent_ref.1), custom_call_target="tpu_custom_call" | custom-call | tf_op jit(solution)/shard_map/pallas_call | solution.py:285
  1.4 15.4 %all_to_all.5 = bf16[16,8,512]{2,1,0:T(8,128)(2,1)} all-to-all(bf16[16,8,512]{2,1,0:T(8,128)(2,1)} %shard_map.82), channel_id=1, replica_groups=mesh['groups'=2,'tm'=16] {'tm'}, dimensions={0} | all-to-all | bytes 262144 | tf_op jit(solution)/shard_map/all_to_all | solution.py:290
  16.9 22.6 %shard_map.83 = bf16[4,512,384]{2,1,0:T(8,128)(2,1)} custom-call(bf16[128,512]{1,0:T(8,128)(2,1)} %bitcast.7, bf16[432,384]{1,0:T(8,128)(2,1)} %bitcast.8, f32[384]{0:T(512)} %bin_ref.1, f32[384]{0:T(512)} %gain_ref.1, bf16[10368,384]{1,0:T(8,128)(2,1)} %bitcast.5, f32[384]{0:T(512)} %bmid_ref.1, bf16[1152,768]{1,0:T(8,128)(2,1)} %bitcast.6, f32[768]{0:T(1024)} %btime_ref.1), custom_call_target="tpu_custom_call" | custom-call | tf_op jit(solution)/shard_map/pallas_call | solution.py:294
